TPU v7x, 256 devices: a whole 4x4x8 slice. The times are simulated.
256 devices in a mesh: tile: 4 (over x), morton: 64 (over z, y, core).
Axes of the slice: x: 4, y: 4, z: 8, core: 2. Of those that a mesh axis runs over, the one named last changes fastest.
Arguments:
- features: bfloat16 [4, 262144, 128], P('tile', 'morton'), may hold values from -6 to 6
- neighbours: int32 [4, 262144, 27], P('tile', 'morton'), may hold values from -1 to 2048, as said below
- counts: int32 [4, 32768], P('tile', 'morton'), may hold values from 1 to 8
- owner: int32 [4, 32768], P('tile', 'morton'), may hold values from 0 to 63, as said below
- slot: int32 [4, 32768], P('tile', 'morton'), may hold values from 0 to 511, as said below
- coarse_neighbours: int32 [4, 32768, 27], P('tile', 'morton'), may hold values from -1 to 2047, as said below
- w_first: bfloat16 [3456, 128], replicated, may hold values from -0.109375 to 0.109375
- w_second: bfloat16 [3456, 128], replicated, may hold values from -0.109375 to 0.109375
- w_down: bfloat16 [1024, 256], replicated, may hold values from -0.1875 to 0.1875
- w_coarse: bfloat16 [6912, 256], replicated, may hold values from -0.078125 to 0.078125
- gain_first: float32 [128], replicated, may hold values from 0.1 to 1.9
- gain_second: float32 [128], replicated, may hold values from 0.1 to 1.9
- gain_down: float32 [256], replicated, may hold values from 0.1 to 1.9
- gain_coarse: float32 [256], replicated, may hold values from 0.1 to 1.9
Outputs:
- fine_out: bfloat16 [4, 262144, 128], P('tile', 'morton')
- coarse_out: bfloat16 [4, 32768, 256], P('tile', 'morton')
Inputs may be any that keep to these rules, and one draw needn't show every extreme that they name: `neighbours`: entry k of octant r's list is -1 for an absent neighbour, else the neighbour's row minus r plus 1024, and the neighbour lies in the same tile; entry 13 is 1024 (r itself). Block b's first counts octants are real, the rest padding. A block's parent is owned by its own device or by the next or previous Morton index of its tile; a device's blocks with a lower owner form a run at the start of its range, those with a higher owner a run at the end. At most 64 blocks of one device have a given other owner, and in every tile some device hands exactly 64 to a neighbour. Within a tile the pairs (owner, slot) are all distinct, so every parent row is filled exactly once. `coarse_neighbours`: rows are numbered t * 512 + s over the parents of the four tiles with the same Morton range, -1 for an absent neighbour; entry 13 is the parent itself. Most entries lie in the parent's own tile; parents on a tile border have some entries in another tile.
All inputs are finite; a program needn't handle non-finite values.
Results may differ from a plain program's by a relative error of at most 0.009.
Values may be sent and summed in bfloat16 or wider, within the bound.
A program may use at most 128 MiB of HBM per device.

v0:
```python
import functools

import jax
import jax.numpy as jnp
from jax import lax
from jax.experimental import pallas as pl
from jax.experimental.pallas import tpu as pltpu
from jax.sharding import PartitionSpec as P

K = 27
TILE = 128
GROUPS = TILE // 16
PAD = 8
EPS = 1e-05
VMEM_LIMIT = 58 * 2**20


def shifted(value, axis, steps):
    count = lax.axis_size(axis)
    initial, last = (max(0, -steps), min(count, count - steps))
    return lax.ppermute(value, axis, [(source, source + steps) for source in range(initial, last)])


def sublane_masks():
    sub = lax.broadcasted_iota(jnp.int32, (8, 128), 0)
    return [sub == i for i in range(8)]


def gather_group(idx_ref, tables, dst_ref, tile, sub, masks):
    halves = len(tables)
    width = 128 * halves
    for k in range(K):
        refs = idx_ref.at[pl.ds(tile * (K * TILE) + k * TILE + sub * 16, 16)]
        parts = [[], []]
        rows = [[None] * 8 for _ in range(2)]
        for h in range(2):
            for i in range(8):
                rows[h][i] = refs[h * 8 + i]
        for n, (table, base) in enumerate(tables):
            both = []
            for h in range(2):
                acc = None
                for i in range(8):
                    v = table[pl.ds(rows[h][i] + (base + PAD - i), 8), :]
                    acc = v if acc is None else jnp.where(masks[i], v, acc)
                both.append(acc)
            col = (k % 4) * width + n * 128
            dst_ref[k // 4, pl.ds(pl.multiple_of(sub * 16, 16), 16), col : col + 128] = jnp.concatenate(
                both, 0
            ).astype(jnp.bfloat16)


def run_tiles(idx_ref, tables, w_ref, ga, gb, acc_ref, pairs, first_tile, masks, epilogue):
    def half(tile, dst, src):
        def body(j, _):
            acc_ref[...] += jnp.dot(src[j], w_ref[j], preferred_element_type=jnp.float32)
            gather_group(idx_ref, tables, dst, tile, j, masks)
            return 0

        lax.fori_loop(0, GROUPS, body, 0)
        epilogue(jnp.maximum(first_tile + tile - 1, 0))
        acc_ref[...] = jnp.zeros_like(acc_ref)

    def pair(p, _):
        half(2 * p, ga, gb)
        half(2 * p + 1, gb, ga)
        return 0

    lax.fori_loop(0, pairs, pair, 0)


def drain(w_ref, gb, acc_ref):
    def body(j, _):
        acc_ref[...] += jnp.dot(gb[j], w_ref[j], preferred_element_type=jnp.float32)
        return 0

    lax.fori_loop(0, GROUPS, body, 0)


def pad_weight(w_in, w_ref, width):
    for c in range(7):
        rows = 4 * width if c < 6 else 3 * width
        w_ref[c, :rows, :] = w_in[c * 4 * width : c * 4 * width + rows, :]
    w_ref[6, 3 * width :, :] = jnp.zeros((width, w_ref.shape[2]), w_ref.dtype)
    w_ref[7, :, :] = jnp.zeros((4 * width, w_ref.shape[2]), w_ref.dtype)


def zero_buffers(ga, gb, acc_ref, width):
    for g in (ga, gb):
        g[6, :, 3 * width :] = jnp.zeros((TILE, width), g.dtype)
        g[7, :, :] = jnp.zeros((TILE, 4 * width), g.dtype)
    acc_ref[...] = jnp.zeros_like(acc_ref)


def normed(h, gain):
    return h * lax.rsqrt(jnp.mean(h * h, axis=-1, keepdims=True) + EPS) * gain


def conv_kernel(
    second,
    idx_ref,
    counts_ref,
    lo_ref,
    mid_ref,
    hi_ref,
    w_in,
    gain_ref,
    *rest,
):
    if second:
        x_ref, wd_ref, gain_down_ref, out_ref, down_ref, table, w_ref, ga, gb, acc_ref, fine_ref = rest
    else:
        out_ref, table, w_ref, ga, gb, acc_ref = rest
    step = pl.program_id(0)
    masks = sublane_masks()
    sub16 = lax.broadcasted_iota(jnp.int32, (8, 128), 0)

    @pl.when(step == 0)
    def _():
        table[:PAD, :] = jnp.zeros((PAD, 128), jnp.float32)
        table[pl.ds(PAD, 1024), :] = lo_ref[...].astype(jnp.float32)
        table[pl.ds(PAD + 1024, 4096), :] = mid_ref[...].astype(jnp.float32)
        table[pl.ds(PAD + 5120, 1024), :] = hi_ref[...].astype(jnp.float32)
        pad_weight(w_in, w_ref, 128)
        zero_buffers(ga, gb, acc_ref, 128)

    def epilogue(tile):
        gain = gain_ref[...]
        for i in range(GROUPS):
            h = normed(acc_ref[i * 16 : (i + 1) * 16, :], gain)
            row = pl.multiple_of(tile * TILE + i * 16, 16)
            if second:
                h = x_ref[pl.ds(row, 16), :].astype(jnp.float32) + h
            valid = jnp.concatenate(
                [sub16 < counts_ref[tile * GROUPS * 2 + 2 * i], sub16 < counts_ref[tile * GROUPS * 2 + 2 * i + 1]], 0
            )
            value = jnp.where(valid, jnp.maximum(h, 0.0), 0.0).astype(jnp.bfloat16)
            out_ref[pl.ds(row, 16), :] = value
            if second:
                fine_ref[pl.ds(row, 16), :] = value.astype(jnp.float32)

    run_tiles(idx_ref, ((table, 0),), w_ref, ga, gb, acc_ref, 4, step * 8, masks, epilogue)

    @pl.when(step == 3)
    def _():
        drain(w_ref, gb, acc_ref)
        epilogue(31)
        if second:

            def down(c, _):
                total = jnp.zeros((64, 256), jnp.float32)
                for j in range(8):
                    child = fine_ref[pl.ds(c * 512 + j, 64, stride=8), :].astype(jnp.bfloat16)
                    total += jnp.dot(child, wd_ref[j * 128 : (j + 1) * 128, :], preferred_element_type=jnp.float32)
                value = jnp.maximum(normed(total, gain_down_ref[...]), 0.0)
                down_ref[pl.ds(pl.multiple_of(c * 64, 64), 64), :] = value.astype(jnp.bfloat16)
                return 0

            lax.fori_loop(0, 8, down, 0)


def whole(shape):
    return pl.BlockSpec(shape, lambda i: (0,) * len(shape))


def conv(second, idx, counts, lo, mid, hi, w, gain, *more):
    specs = [
        pl.BlockSpec((8 * K * TILE,), lambda i: (i,), memory_space=pltpu.SMEM),
        pl.BlockSpec(memory_space=pltpu.SMEM),
    ] + [whole(a.shape) for a in (lo, mid, hi, w, gain) + more]
    out_shape = [jax.ShapeDtypeStruct((4096, 128), jnp.bfloat16)]
    scratch = [
        pltpu.VMEM((PAD + 6144 + 8, 128), jnp.float32),
        pltpu.VMEM((8, 512, 128), jnp.bfloat16),
        pltpu.VMEM((8, TILE, 512), jnp.bfloat16),
        pltpu.VMEM((8, TILE, 512), jnp.bfloat16),
        pltpu.VMEM((TILE, 128), jnp.float32),
    ]
    if second:
        out_shape.append(jax.ShapeDtypeStruct((512, 256), jnp.bfloat16))
        scratch.append(pltpu.VMEM((4096, 128), jnp.float32))
    return pl.pallas_call(
        functools.partial(conv_kernel, second),
        grid=(4,),
        in_specs=specs,
        out_specs=[whole(s.shape) for s in out_shape],
        out_shape=out_shape,
        scratch_shapes=scratch,
        name="conv_second" if second else "conv_first",
        compiler_params=pltpu.CompilerParams(vmem_limit_bytes=VMEM_LIMIT),
    )(idx, counts, lo, mid, hi, w, gain, *more)


def place_kernel(pos_ref, own_ref, below_ref, above_ref, out_ref, src, dst):
    src[:512, :] = own_ref[:, :128].astype(jnp.float32)
    src[512:576, :] = below_ref[:, :128].astype(jnp.float32)
    src[576:640, :] = above_ref[:, :128].astype(jnp.float32)
    src[640:1152, :] = own_ref[:, 128:].astype(jnp.float32)
    src[1152:1216, :] = below_ref[:, 128:].astype(jnp.float32)
    src[1216:1280, :] = above_ref[:, 128:].astype(jnp.float32)

    def body(g, _):
        for i in range(16):
            at = pos_ref[g * 16 + i]
            dst[pl.ds(at, 1), :] = src[pl.ds(g * 16 + i, 1), :]
            dst[pl.ds(at + 520, 1), :] = src[pl.ds(g * 16 + i + 640, 1), :]
        return 0

    lax.fori_loop(0, 40, body, 0)
    out_ref[:, :128] = dst[:512, :].astype(jnp.bfloat16)
    out_ref[:, 128:] = dst[520:1032, :].astype(jnp.bfloat16)


def place(pos, own, below, above):
    return pl.pallas_call(
        place_kernel,
        in_specs=[pl.BlockSpec(memory_space=pltpu.SMEM)] + [pl.BlockSpec(memory_space=pltpu.VMEM)] * 3,
        out_specs=pl.BlockSpec(memory_space=pltpu.VMEM),
        out_shape=jax.ShapeDtypeStruct((512, 256), jnp.bfloat16),
        scratch_shapes=[pltpu.VMEM((1280, 128), jnp.float32), pltpu.VMEM((1040, 128), jnp.float32)],
        name="place",
    )(pos, own, below, above)


HALF = 2048 + 16


def coarse_kernel(idx_ref, pool_ref, own_ref, w_in, gain_ref, out_ref, table, w_ref, ga, gb, acc_ref):
    masks = sublane_masks()
    table[:PAD, :] = jnp.zeros((PAD, 128), jnp.float32)
    table[HALF : HALF + PAD, :] = jnp.zeros((PAD, 128), jnp.float32)
    table[pl.ds(PAD, 2048), :] = pool_ref[:, :128].astype(jnp.float32)
    table[pl.ds(HALF + PAD, 2048), :] = pool_ref[:, 128:].astype(jnp.float32)
    pad_weight(w_in, w_ref, 256)
    zero_buffers(ga, gb, acc_ref, 256)

    def epilogue(tile):
        for i in range(GROUPS):
            h = normed(acc_ref[i * 16 : (i + 1) * 16, :], gain_ref[...])
            row = pl.multiple_of(tile * TILE + i * 16, 16)
            h = own_ref[pl.ds(row, 16), :].astype(jnp.float32) + h
            out_ref[pl.ds(row, 16), :] = jnp.maximum(h, 0.0).astype(jnp.bfloat16)

    run_tiles(idx_ref, ((table, 0), (table, HALF)), w_ref, ga, gb, acc_ref, 2, 0, masks, epilogue)
    drain(w_ref, gb, acc_ref)
    epilogue(3)


def coarse(idx, pool, own, w, gain):
    return pl.pallas_call(
        coarse_kernel,
        in_specs=[pl.BlockSpec(memory_space=pltpu.SMEM)] + [pl.BlockSpec(memory_space=pltpu.VMEM)] * 4,
        out_specs=pl.BlockSpec(memory_space=pltpu.VMEM),
        out_shape=jax.ShapeDtypeStruct((512, 256), jnp.bfloat16),
        scratch_shapes=[
            pltpu.VMEM((2 * HALF, 128), jnp.float32),
            pltpu.VMEM((8, 1024, 256), jnp.bfloat16),
            pltpu.VMEM((8, TILE, 1024), jnp.bfloat16),
            pltpu.VMEM((8, TILE, 1024), jnp.bfloat16),
            pltpu.VMEM((TILE, 256), jnp.float32),
        ],
        name="coarse",
        compiler_params=pltpu.CompilerParams(vmem_limit_bytes=VMEM_LIMIT),
    )(idx, pool, own, w, gain)


def by_tiles(index):
    rows = index.shape[1]
    return index.reshape(K, rows // TILE, TILE).transpose(1, 0, 2).reshape(-1)


def shards(
    features,
    neighbours,
    counts,
    owner,
    slot,
    coarse_neighbours,
    w_first,
    w_second,
    w_down,
    w_coarse,
    gain_first,
    gain_second,
    gain_down,
    gain_coarse,
):
    lane_ids = jnp.arange(8, dtype=jnp.int32)
    valid = lane_ids[None, :] < counts[0][:, None]
    field = jnp.where(valid[:, :, None], features[0].reshape(512, 8, 128), 0).astype(jnp.bfloat16).reshape(4096, 128)
    by_offset = neighbours[0].T
    local = by_offset + jnp.arange(4096, dtype=jnp.int32)[None, :]
    idx = by_tiles(jnp.where(by_offset < 0, -1, local))
    coarse_idx = by_tiles(coarse_neighbours[0].T)

    me = lax.axis_index("morton")
    destination, plus = owner[0], slot[0] + 1
    own_at = jnp.where(destination == me, plus, 0)
    below_at = shifted(jnp.where(destination == me + 1, plus, 0)[448:], "morton", 1)
    above_at = shifted(jnp.where(destination == me - 1, plus, 0)[:64], "morton", -1)
    at = jnp.concatenate([own_at, below_at, above_at])
    at = jnp.where(at > 0, at - 1, 512)

    def halo(v):
        return shifted(v[3072:], "morton", 1), shifted(v[:1024], "morton", -1)

    lo, hi = halo(field)
    (act,) = conv(False, idx, counts[0], lo, field, hi, w_first, gain_first[None])
    lo, hi = halo(act)
    fine, rows = conv(
        True, idx, counts[0], lo, act, hi, w_second, gain_second[None], field, w_down, gain_down[None]
    )
    below, above = shifted(rows[448:], "morton", 1), shifted(rows[:64], "morton", -1)
    parents = place(at, rows, below, above)
    pool = lax.all_gather(parents, "tile", axis=0, tiled=True)
    out = coarse(coarse_idx, pool, parents, w_coarse, gain_coarse[None])
    return fine[None], out[None]


def solution(mesh):
    split = P("tile", "morton", None)
    flat = P("tile", "morton")
    in_specs = (split, split, flat, flat, flat, split) + (P(),) * 8
    return jax.shard_map(shards, mesh=mesh, in_specs=in_specs, out_specs=(split, split), check_vma=False)
```

profile of v0, /device:TPU:120, one launch (start us, length us, event | category | flops | bytes accessed | tf_op | source)
XLA Modules:
  0.0 381.5 jit_solution(6697602595294749611)
XLA Ops:
  7.2 0.0 copy-start
  7.2 0.0 copy-start.1
  7.2 0.0 all-gather.2.cloned.1.call-start
  7.2 0.9 iota_compare_fusion
  8.2 3.0 bitcast_select_fusion.1
  11.2 1.9 collective-permute-start
  13.2 3.6 collective-permute-start.1
  16.8 0.2 lt.32
  17.0 0.0 copy-done
  17.0 2.9 bitcast_select_fusion.mid_ref.rest_0_
  19.9 0.0 copy-done.1
  19.9 0.3 fusion
  20.2 0.1 copy.20
  20.4 0.0 copy-start.9
  20.4 0.0 copy-start.10
  20.4 0.3 copy.30
  20.7 0.8 reshape.66.idx_ref
  21.5 0.0 collective-permute-done.lo_ref
  21.5 0.0 copy-start.4
  21.5 0.0 collective-permute-done.1.hi_ref
  21.5 0.0 copy-start.5
  21.5 0.7 copy-done.4
  22.2 0.1 copy-done.5
  22.3 130.6 %conv_first.1.mid_ref = bf16[4096,128]{1,0:T(8,128)(2,1)} custom-call(s32[110592]{0:T(1024)} %reshape.66.idx_ref, s32[512]{0:T(512)} %bitcast.50, bf16[1024,128]{1,0:T(8,128)(2,1)} %copy-done.4, bf16[4096,128]{1,0:T(8,128)(2,1)} %bitcast_select_fusion.mid_ref.rest_0_, bf16[1024,128]{1,0:T(8,128)(2,1)} %copy-done.5, bf16[3456,128]{1,0:T(8,128)(2,1)} %w_in.3, ...), custom_call_target="tpu_custom_call" | custom-call | tf_op jit(solution)/shard_map/conv_first/pallas_call | solution.py:182
  152.8 0.0 copy-start.6
  152.8 1.1 fusion.3
  153.9 7.4 %collective-permute-start.2 = (bf16[1024,128]{1,0:T(8,128)(2,1)S(1)}, bf16[1024,128]{1,0:T(8,128)(2,1)S(1)}, u32[]{:S(2)}, u32[]{:S(2)}) collective-permute-start(bf16[1024,128]{1,0:T(8,128)(2,1)S(1)} %get-tuple-element.7), channel_id=1, source_target_pairs={{0,1},{1,2},{2,3},{3,4},{4,5},{5,6},{6,7},{7,8},{8,9},{9,10},{10,1... | collective-permute-start | bytes 786440 | tf_op jit(solution)/shard_map/ppermute | solution.py:21
  161.3 1.9 collective-permute-start.3
  163.3 0.0 copy-done.9
  163.3 0.0 copy-done.10
  163.3 0.1 fusion.1
  163.4 2.6 collective-permute-start.4
  166.0 2.9 collective-permute-start.5
  168.9 0.0 collective-permute-done.2.lo_ref
  169.0 0.0 copy-start.2
  169.0 0.0 collective-permute-done.3.hi_ref
  169.0 0.0 copy-start.3
  169.0 0.7 copy-done.2
  169.7 0.1 copy-done.3
  169.7 133.4 %conv_second.1 = (bf16[4096,128]{1,0:T(8,128)(2,1)}, bf16[512,256]{1,0:T(8,128)(2,1)}) custom-call(s32[110592]{0:T(1024)} %reshape.66.idx_ref, s32[512]{0:T(512)} %bitcast.51, bf16[1024,128]{1,0:T(8,128)(2,1)} %copy-done.2, bf16[4096,128]{1,0:T(8,128)(2,1)} %conv_first.1.mid_ref, bf16[1024,128]{1,0:T(8,128)(2,1)} %copy-done.3, bf16[3456,128]{1,0:T(8,128)(2,1)} %w_in.4, ...), custom_call_target="tpu_custom_call" | custom-call | tf_op jit(solution)/shard_map/conv_second/pallas_call | solution.py:182
  303.2 0.8 fusion.4
  303.9 5.9 %collective-permute-start.6 = (bf16[64,256]{1,0:T(8,128)(2,1)S(1)}, bf16[64,256]{1,0:T(8,128)(2,1)S(1)}, u32[]{:S(2)}, u32[]{:S(2)}) collective-permute-start(bf16[64,256]{1,0:T(8,128)(2,1)S(1)} %get-tuple-element.11), channel_id=1, source_target_pairs={{0,1},{1,2},{2,3},{3,4},{4,5},{5,6},{6,7},{7,8},{8,9},{9,10},{10,1... | collective-permute-start | bytes 98312 | tf_op jit(solution)/shard_map/ppermute | solution.py:21
  309.9 1.9 collective-permute-start.7
  311.8 0.0 collective-permute-done.4
  311.8 0.0 collective-permute-done.5
  311.8 0.7 add_select_fusion.pos_ref
  312.5 0.0 collective-permute-done.6.below_ref
  312.5 0.0 copy-start.7
  312.5 5.0 %collective-permute-done.7.above_ref = bf16[64,256]{1,0:T(8,128)(2,1)S(1)} collective-permute-done((bf16[64,256]{1,0:T(8,128)(2,1)S(1)}, bf16[64,256]{1,0:T(8,128)(2,1)S(1)}, u32[]{:S(2)}, u32[]{:S(2)}) %collective-permute-start.7) | collective-permute-done | bytes 32800 | tf_op jit(solution)/shard_map/ppermute | solution.py:21
  317.5 0.0 copy-done.7
  317.5 0.0 copy-start.8
  317.5 0.6 copy-done.8
  318.1 2.6 place.1.own_ref
  320.7 0.0 all-gather.2.cloned.1.call-update
  320.8 0.0 copy-done.6
  320.8 0.6 reshape.68.idx_ref
  321.5 30.4 %all-gather.2.cloned.1.call-done.pool_ref = bf16[2048,256]{1,0:T(8,128)(2,1)} async-done(((bf16[512,256]{1,0:T(8,128)(2,1)}), bf16[2048,256]{1,0:T(8,128)(2,1)}) %all-gather.2.cloned.1.call-update) | async-done | bytes 1048592 | tf_op jit(solution)/shard_map/all_gather | solution.py:315
  351.8 22.8 %coarse.1 = bf16[512,256]{1,0:T(8,128)(2,1)} custom-call(s32[13824]{0:T(1024)} %reshape.68.idx_ref, bf16[2048,256]{1,0:T(8,128)(2,1)} %all-gather.2.cloned.1.call-done.pool_ref, bf16[512,256]{1,0:T(8,128)(2,1)} %place.1.own_ref, bf16[6912,256]{1,0:T(8,128)(2,1)} %w_in.5, f32[1,256]{1,0:T(1,128)} %bitcast.54), custom_call_target="tpu_custom_call" | custom-call | tf_op jit(solution)/shard_map/coarse/pallas_call | solution.py:250
  (6 shorter events, 0.1 us)
Async XLA Ops:
  7.2 9.8 %copy-start = (bf16[1,4096,128]{2,1,0:T(8,128)(2,1)S(1)}, bf16[1,4096,128]{2,1,0:T(8,128)(2,1)}, u32[]{:S(2)}) copy-start(bf16[1,4096,128]{2,1,0:T(8,128)(2,1)} %param.14) | copy-start | bytes 3145732
  7.2 12.7 %copy-start.1 = (s32[1,4096,27]{1,0,2:T(1,128)S(1)}, s32[1,4096,27]{1,0,2:T(1,128)}, u32[]{:S(2)}) copy-start(s32[1,4096,27]{1,0,2:T(1,128)} %param.15) | copy-start | bytes 1327108
  7.2 344.6 %all-gather.2.cloned.1.call-start = ((), (), s32[]{:S(2)}) async-start(), calls=%async_computation | async-start | bytes 1310720 | tf_op jit(solution)/shard_map/all_gather | solution.py:315
  11.2 10.2 %collective-permute-start = (bf16[1024,128]{1,0:T(8,128)(2,1)S(1)}, bf16[1024,128]{1,0:T(8,128)(2,1)S(1)}, u32[]{:S(2)}, u32[]{:S(2)}) collective-permute-start(bf16[1024,128]{1,0:T(8,128)(2,1)S(1)} %get-tuple-element.9), channel_id=1, source_target_pairs={{0,1},{1,2},{2,3},{3,4},{4,5},{5,6},{6,7},{7,8},{8,9},{9,10},{10,1... | collective-permute-start | bytes 786440 | tf_op jit(solution)/shard_map/ppermute | solution.py:21
  13.2 8.3 %collective-permute-start.1 = (bf16[1024,128]{1,0:T(8,128)(2,1)S(1)}, bf16[1024,128]{1,0:T(8,128)(2,1)S(1)}, u32[]{:S(2)}, u32[]{:S(2)}) collective-permute-start(bf16[1024,128]{1,0:T(8,128)(2,1)S(1)} %get-tuple-element.8), channel_id=1, source_target_pairs={{1,0},{2,1},{3,2},{4,3},{5,4},{6,5},{7,6},{8,7},{9,8},{10,9},{11,1... | collective-permute-start | bytes 786440 | tf_op jit(solution)/shard_map/ppermute | solution.py:21
  20.4 142.9 %copy-start.9 = (s32[1,512]{1,0:T(1,128)S(1)}, s32[1,512]{1,0:T(1,128)}, u32[]{:S(2)}) copy-start(s32[1,512]{1,0:T(1,128)} %param.17) | copy-start | bytes 6148
  20.4 142.9 %copy-start.10 = (s32[1,512]{1,0:T(1,128)S(1)}, s32[1,512]{1,0:T(1,128)}, u32[]{:S(2)}) copy-start(s32[1,512]{1,0:T(1,128)} %param.18) | copy-start | bytes 6148
  21.5 0.7 copy-start.4
  21.5 0.8 copy-start.5
  152.8 168.0 %copy-start.6 = (s32[1,512,27]{1,0,2:T(1,128)S(1)}, s32[1,512,27]{1,0,2:T(1,128)}, u32[]{:S(2)}) copy-start(s32[1,512,27]{1,0,2:T(1,128)} %param.19) | copy-start | bytes 165892
  153.9 15.1 %collective-permute-start.2 = (bf16[1024,128]{1,0:T(8,128)(2,1)S(1)}, bf16[1024,128]{1,0:T(8,128)(2,1)S(1)}, u32[]{:S(2)}, u32[]{:S(2)}) collective-permute-start(bf16[1024,128]{1,0:T(8,128)(2,1)S(1)} %get-tuple-element.7), channel_id=1, source_target_pairs={{0,1},{1,2},{2,3},{3,4},{4,5},{5,6},{6,7},{7,8},{8,9},{9,10},{10,1... | collective-permute-start | bytes 786440 | tf_op jit(solution)/shard_map/ppermute | solution.py:21
  161.3 7.6 %collective-permute-start.3 = (bf16[1024,128]{1,0:T(8,128)(2,1)S(1)}, bf16[1024,128]{1,0:T(8,128)(2,1)S(1)}, u32[]{:S(2)}, u32[]{:S(2)}) collective-permute-start(bf16[1024,128]{1,0:T(8,128)(2,1)S(1)} %get-tuple-element.6), channel_id=1, source_target_pairs={{1,0},{2,1},{3,2},{4,3},{5,4},{6,5},{7,6},{8,7},{9,8},{10,9},{11,1... | collective-permute-start | bytes 786440 | tf_op jit(solution)/shard_map/ppermute | solution.py:21
  163.4 148.4 %collective-permute-start.4 = (s32[64]{0:T(128)S(1)}, s32[64]{0:T(128)S(1)}, u32[]{:S(2)}, u32[]{:S(2)}) collective-permute-start(s32[64]{0:T(128)S(1)} %get-tuple-element.12), channel_id=1, source_target_pairs={{0,1},{1,2},{2,3},{3,4},{4,5},{5,6},{6,7},{7,8},{8,9},{9,10},{10,1... | collective-permute-start | bytes 776 | tf_op jit(solution)/shard_map/ppermute | solution.py:21
  166.0 145.8 %collective-permute-start.5 = (s32[64]{0:T(128)S(1)}, s32[64]{0:T(128)S(1)}, u32[]{:S(2)}, u32[]{:S(2)}) collective-permute-start(s32[64]{0:T(128)S(1)} %get-tuple-element.13), channel_id=1, source_target_pairs={{1,0},{2,1},{3,2},{4,3},{5,4},{6,5},{7,6},{8,7},{9,8},{10,9},{11,1... | collective-permute-start | bytes 776 | tf_op jit(solution)/shard_map/ppermute | solution.py:21
  169.0 0.7 copy-start.2
  169.0 0.8 copy-start.3
  303.9 8.6 %collective-permute-start.6 = (bf16[64,256]{1,0:T(8,128)(2,1)S(1)}, bf16[64,256]{1,0:T(8,128)(2,1)S(1)}, u32[]{:S(2)}, u32[]{:S(2)}) collective-permute-start(bf16[64,256]{1,0:T(8,128)(2,1)S(1)} %get-tuple-element.11), channel_id=1, source_target_pairs={{0,1},{1,2},{2,3},{3,4},{4,5},{5,6},{6,7},{7,8},{8,9},{9,10},{10,1... | collective-permute-start | bytes 98312 | tf_op jit(solution)/shard_map/ppermute | solution.py:21
  309.9 7.7 %collective-permute-start.7 = (bf16[64,256]{1,0:T(8,128)(2,1)S(1)}, bf16[64,256]{1,0:T(8,128)(2,1)S(1)}, u32[]{:S(2)}, u32[]{:S(2)}) collective-permute-start(bf16[64,256]{1,0:T(8,128)(2,1)S(1)} %get-tuple-element.10), channel_id=1, source_target_pairs={{1,0},{2,1},{3,2},{4,3},{5,4},{6,5},{7,6},{8,7},{9,8},{10,9},{11,1... | collective-permute-start | bytes 98312 | tf_op jit(solution)/shard_map/ppermute | solution.py:21
  312.5 5.0 %copy-start.7 = (bf16[64,256]{1,0:T(8,128)(2,1)}, bf16[64,256]{1,0:T(8,128)(2,1)S(1)}, u32[]{:S(2)}) copy-start(bf16[64,256]{1,0:T(8,128)(2,1)S(1)} %collective-permute-done.6.below_ref) | copy-start | bytes 98308
  317.5 0.6 copy-start.8
Sparse Core Ops, SparseCore 0:
  320.9 30.8 all-gather.1
where the time goes:
time: 383 us; the launch traced here: 381 us
  Pallas kernels  289 us (75%)
  waiting for transfers between devices  35.4 us (9%)
  starting transfers between devices  28.4 us (7%)
  between operations  14.3 us (4%)
  other arithmetic  7.92 us (2%)
  local copies, waits for them, and re-layouts  6.07 us (2%)
    pallas_call x2, Pallas kernels, conv(): pl.pallas_call(functools.partial(conv_kernel, second), grid=(4,), in_spec...  264 us
    all_gather x1, waiting for transfers between devices, shards(): pool = lax.all_gather(parents, 'tile', axis=0, tiled=True)  30.4 us
    ppermute x8, starting transfers between devices, shifted(): lax.ppermute(value, axis, [(source, source + steps) for source in range(i...  28.3 us
    pallas_call x1, Pallas kernels, coarse(): pl.pallas_call(coarse_kernel, in_specs=[pl.BlockSpec(memory_space=pltpu.S...  22.8 us
  transfers between devices with their start and end apart: 9, of which 2 were waited for; matrix products, arithmetic and copies ran while one was open for 2% of the time, Pallas kernels for 35%

commit v1 on v0

v1 whole, which is shorter than its diff:
```python
import functools

import jax
import jax.numpy as jnp
from jax import lax
from jax.experimental import pallas as pl
from jax.experimental.pallas import tpu as pltpu
from jax.sharding import PartitionSpec as P

K = 27
TILE = 128
GROUPS = TILE // 16
PAD = 8
EPS = 1e-05
VMEM_LIMIT = 58 * 2**20


def shifted(value, axis, steps):
    count = lax.axis_size(axis)
    initial, last = (max(0, -steps), min(count, count - steps))
    return lax.ppermute(value, axis, [(source, source + steps) for source in range(initial, last)])


def sublane_masks():
    sub = lax.broadcasted_iota(jnp.int32, (8, 128), 0)
    return [sub == i for i in range(8)]


def gather_rows(idx_ref, tables, dst_ref, tiles, masks):
    width = 128 * len(tables)

    def body(g, _):
        base_ref = idx_ref.at[pl.ds((g // GROUPS) * (K * TILE) + (g % GROUPS) * 16, (K - 1) * TILE + 16)]
        for k in range(K):
            both = [[] for _ in tables]
            for h in range(2):
                at = base_ref.at[pl.ds(k * TILE + h * 8, 8)]
                acc = [None for _ in tables]
                for i in range(8):
                    row = at[i]
                    for n, (table, base) in enumerate(tables):
                        v = table[pl.ds(row + (base + PAD - i), 8), :]
                        acc[n] = v if i == 0 else jnp.where(masks[i], v, acc[n])
                for n in range(len(tables)):
                    both[n].append(acc[n])
            for n in range(len(tables)):
                col = k * width + n * 128
                dst_ref[pl.ds(pl.multiple_of(g * 16, 16), 16), col : col + 128] = jnp.concatenate(
                    both[n], 0
                ).astype(jnp.bfloat16)
        return 0

    lax.fori_loop(0, tiles * GROUPS, body, 0)


def normed(h, gain):
    return h * lax.rsqrt(jnp.mean(h * h, axis=-1, keepdims=True) + EPS) * gain


def conv_kernel(
    second,
    idx_ref,
    counts_ref,
    lo_ref,
    mid_ref,
    hi_ref,
    w_in,
    gain_ref,
    *rest,
):
    if second:
        x_ref, wd_ref, gain_down_ref, out_ref, down_ref, table, gathered, acc_ref, fine_ref = rest
    else:
        out_ref, table, gathered, acc_ref = rest
    step = pl.program_id(0)
    masks = sublane_masks()
    sub16 = lax.broadcasted_iota(jnp.int32, (8, 128), 0)

    @pl.when(step == 0)
    def _():
        table[:PAD, :] = jnp.zeros((PAD, 128), jnp.float32)
        table[pl.ds(PAD, 1024), :] = lo_ref[...].astype(jnp.float32)
        table[pl.ds(PAD + 1024, 4096), :] = mid_ref[...].astype(jnp.float32)
        table[pl.ds(PAD + 5120, 1024), :] = hi_ref[...].astype(jnp.float32)

    gather_rows(idx_ref, ((table, 0),), gathered, 8, masks)
    acc_ref[...] = jnp.dot(gathered[...], w_in[...], preferred_element_type=jnp.float32)

    def epilogue(tile, _):
        gain = gain_ref[...]
        for i in range(GROUPS):
            h = normed(acc_ref[pl.ds(pl.multiple_of(tile * TILE + i * 16, 16), 16), :], gain)
            row = pl.multiple_of(step * 1024 + tile * TILE + i * 16, 16)
            if second:
                h = x_ref[pl.ds(row, 16), :].astype(jnp.float32) + h
            block = step * 128 + tile * GROUPS * 2 + 2 * i
            valid = jnp.concatenate([sub16 < counts_ref[block], sub16 < counts_ref[block + 1]], 0)
            value = jnp.where(valid, jnp.maximum(h, 0.0), 0.0).astype(jnp.bfloat16)
            out_ref[pl.ds(row, 16), :] = value
            if second:
                fine_ref[pl.ds(row, 16), :] = value.astype(jnp.float32)
        return 0

    lax.fori_loop(0, 8, epilogue, 0)

    if second:

        @pl.when(step == 3)
        def _():

            def down(c, _):
                total = jnp.zeros((64, 256), jnp.float32)
                for j in range(8):
                    child = fine_ref[pl.ds(c * 512 + j, 64, stride=8), :].astype(jnp.bfloat16)
                    total += jnp.dot(child, wd_ref[j * 128 : (j + 1) * 128, :], preferred_element_type=jnp.float32)
                value = jnp.maximum(normed(total, gain_down_ref[...]), 0.0)
                down_ref[pl.ds(pl.multiple_of(c * 64, 64), 64), :] = value.astype(jnp.bfloat16)
                return 0

            lax.fori_loop(0, 8, down, 0)


def whole(shape):
    return pl.BlockSpec(shape, lambda i: (0,) * len(shape))


def conv(second, idx, counts, lo, mid, hi, w, gain, *more):
    specs = [
        pl.BlockSpec((8 * K * TILE,), lambda i: (i,), memory_space=pltpu.SMEM),
        pl.BlockSpec(memory_space=pltpu.SMEM),
    ] + [whole(a.shape) for a in (lo, mid, hi, w, gain) + more]
    out_shape = [jax.ShapeDtypeStruct((4096, 128), jnp.bfloat16)]
    scratch = [
        pltpu.VMEM((PAD + 6144 + 8, 128), jnp.float32),
        pltpu.VMEM((1024, K * 128), jnp.bfloat16),
        pltpu.VMEM((1024, 128), jnp.float32),
    ]
    if second:
        out_shape.append(jax.ShapeDtypeStruct((512, 256), jnp.bfloat16))
        scratch.append(pltpu.VMEM((4096, 128), jnp.float32))
    return pl.pallas_call(
        functools.partial(conv_kernel, second),
        grid=(4,),
        in_specs=specs,
        out_specs=[whole(s.shape) for s in out_shape],
        out_shape=out_shape,
        scratch_shapes=scratch,
        name="conv_second" if second else "conv_first",
        compiler_params=pltpu.CompilerParams(vmem_limit_bytes=VMEM_LIMIT),
    )(idx, counts, lo, mid, hi, w, gain, *more)


HALF = 2048 + 16
NOWHERE = PAD + 2048
REACH = 640


def exchange_kernel(rows_ref, codes_ref, pool_ref, places_ref, send_sem, recv_sem, local_sem):
    tile, me = lax.axis_index("tile"), lax.axis_index("morton")
    tiles, ranges = lax.axis_size("tile"), lax.axis_size("morton")
    above, below = lax.rem(me + 1, ranges), lax.rem(me + ranges - 1, ranges)
    peers = [lax.rem(tile + d, tiles) for d in range(tiles)]

    barrier = pltpu.get_barrier_semaphore()
    partners = [(peers[d], me) for d in range(1, tiles)] + [(peers[d], m) for m in (above, below) for d in range(tiles)]
    for partner in partners:
        pl.semaphore_signal(barrier, inc=1, device_id=partner, device_id_type=pl.DeviceIdType.MESH)
    pl.semaphore_wait(barrier, len(partners))

    copies = []

    def send(src, dst, partner):
        n = len(copies)
        copy = pltpu.make_async_remote_copy(
            src_ref=src,
            dst_ref=dst,
            send_sem=send_sem.at[n],
            recv_sem=recv_sem.at[n],
            device_id=partner,
            device_id_type=pl.DeviceIdType.MESH,
        )
        copy.start()
        copies.append(copy)

    for d in (2, 1, 3):
        send(rows_ref, pool_ref.at[tile, pl.ds(0, 512)], (peers[d], me))
        send(codes_ref.at[0], places_ref.at[0, tile], (peers[d], me))
    for d in range(tiles):
        send(rows_ref.at[pl.ds(448, 64)], pool_ref.at[tile, pl.ds(512, 64)], (peers[d], above))
        send(codes_ref.at[1], places_ref.at[1, tile], (peers[d], above))
        send(rows_ref.at[pl.ds(0, 64)], pool_ref.at[tile, pl.ds(576, 64)], (peers[d], below))
        send(codes_ref.at[1], places_ref.at[2, tile], (peers[d], below))
    own = [
        pltpu.make_async_copy(rows_ref, pool_ref.at[tile, pl.ds(0, 512)], local_sem.at[0]),
        pltpu.make_async_copy(codes_ref.at[0], places_ref.at[0, tile], local_sem.at[1]),
    ]
    for copy in own:
        copy.start()
    for copy in own + copies:
        copy.wait()


def exchange(rows, codes):
    return pl.pallas_call(
        exchange_kernel,
        in_specs=[pl.BlockSpec(memory_space=pl.ANY)] * 2,
        out_specs=[pl.BlockSpec(memory_space=pl.ANY)] * 2,
        out_shape=[
            jax.ShapeDtypeStruct((4, REACH, 256), jnp.bfloat16),
            jax.ShapeDtypeStruct((3, 4, 8, 128), jnp.int32),
        ],
        scratch_shapes=[
            pltpu.SemaphoreType.DMA((22,)),
            pltpu.SemaphoreType.DMA((22,)),
            pltpu.SemaphoreType.DMA((2,)),
        ],
        name="exchange",
        compiler_params=pltpu.CompilerParams(collective_id=0, has_side_effects=True),
    )(rows, codes)


def coarse_kernel(idx_ref, places_ref, pool_ref, w_in, gain_ref, out_ref, table, source, gathered, acc_ref):
    masks = sublane_masks()
    table[:PAD, :] = jnp.zeros((PAD, 128), jnp.float32)
    table[HALF : HALF + PAD, :] = jnp.zeros((PAD, 128), jnp.float32)

    def tile_rows(t, _):
        source[:REACH, :] = pool_ref[t, :, :128].astype(jnp.float32)
        source[REACH:, :] = pool_ref[t, :, 128:].astype(jnp.float32)

        def put(kind, line, col, row):
            for i in range(16):
                at = places_ref[kind, t, line, col + i]
                table[pl.ds(at, 1), :] = source[pl.ds(row + i, 1), :]
                table[pl.ds(at + HALF, 1), :] = source[pl.ds(row + i + REACH, 1), :]

        def own(g, _):
            put(0, g // 8, (g % 8) * 16, pl.multiple_of(g * 16, 16))
            return 0

        lax.fori_loop(0, 32, own, 0)
        for g in range(4):
            put(1, 0, g * 16, 512 + g * 16)
            put(2, 0, 64 + g * 16, 576 + g * 16)
        return 0

    lax.fori_loop(0, 4, tile_rows, 0)
    gather_rows(idx_ref, ((table, 0), (table, HALF)), gathered, 4, masks)
    acc_ref[...] = jnp.dot(gathered[...], w_in[...], preferred_element_type=jnp.float32)
    first = PAD + 512 * lax.axis_index("tile")

    def epilogue(tile, _):
        for i in range(GROUPS):
            row = pl.multiple_of(tile * TILE + i * 16, 16)
            h = normed(acc_ref[pl.ds(row, 16), :], gain_ref[...])
            at = pl.multiple_of(first + row, 8)
            own = jnp.concatenate([table[pl.ds(at, 16), :], table[pl.ds(at + HALF, 16), :]], 1)
            out_ref[pl.ds(row, 16), :] = jnp.maximum(own + h, 0.0).astype(jnp.bfloat16)
        return 0

    lax.fori_loop(0, 4, epilogue, 0)


def coarse(idx, places, pool, w, gain):
    return pl.pallas_call(
        coarse_kernel,
        in_specs=[pl.BlockSpec(memory_space=pltpu.SMEM)] * 2 + [pl.BlockSpec(memory_space=pltpu.VMEM)] * 3,
        out_specs=pl.BlockSpec(memory_space=pltpu.VMEM),
        out_shape=jax.ShapeDtypeStruct((512, 256), jnp.bfloat16),
        scratch_shapes=[
            pltpu.VMEM((2 * HALF, 128), jnp.float32),
            pltpu.VMEM((2 * REACH, 128), jnp.float32),
            pltpu.VMEM((512, K * 256), jnp.bfloat16),
            pltpu.VMEM((512, 256), jnp.float32),
        ],
        name="coarse",
        compiler_params=pltpu.CompilerParams(vmem_limit_bytes=VMEM_LIMIT),
    )(idx, places, pool, w, gain)


def by_tiles(index):
    rows = index.shape[1]
    return index.reshape(K, rows // TILE, TILE).transpose(1, 0, 2).reshape(-1)


def shards(
    features,
    neighbours,
    counts,
    owner,
    slot,
    coarse_neighbours,
    w_first,
    w_second,
    w_down,
    w_coarse,
    gain_first,
    gain_second,
    gain_down,
    gain_coarse,
):
    lane_ids = jnp.arange(8, dtype=jnp.int32)
    valid = lane_ids[None, :] < counts[0][:, None]
    field = jnp.where(valid[:, :, None], features[0].reshape(512, 8, 128), 0).astype(jnp.bfloat16).reshape(4096, 128)
    by_offset = neighbours[0].T
    local = by_offset + jnp.arange(4096, dtype=jnp.int32)[None, :]
    idx = by_tiles(jnp.where(by_offset < 0, -1, local))
    coarse_idx = by_tiles(coarse_neighbours[0].T)

    me = lax.axis_index("morton")
    destination = owner[0]
    at = PAD + 512 * lax.axis_index("tile") + slot[0]

    def handed(to):
        return jnp.where(destination == to, at, NOWHERE)

    edges = jnp.concatenate([handed(me + 1)[448:], handed(me - 1)[:64]])
    codes = jnp.stack([handed(me).reshape(4, 128), jnp.broadcast_to(edges[None], (4, 128))])
    codes = jnp.concatenate([codes, codes], axis=1)

    def halo(v):
        return shifted(v[3072:], "morton", 1), shifted(v[:1024], "morton", -1)

    lo, hi = halo(field)
    (act,) = conv(False, idx, counts[0], lo, field, hi, w_first, gain_first[None])
    lo, hi = halo(act)
    fine, rows = conv(
        True, idx, counts[0], lo, act, hi, w_second, gain_second[None], field, w_down, gain_down[None]
    )
    pool, places = exchange(rows, codes)
    out = coarse(coarse_idx, places, pool, w_coarse, gain_coarse[None])
    return fine[None], out[None]


def solution(mesh):
    split = P("tile", "morton", None)
    flat = P("tile", "morton")
    in_specs = (split, split, flat, flat, flat, split) + (P(),) * 8
    return jax.shard_map(shards, mesh=mesh, in_specs=in_specs, out_specs=(split, split), check_vma=False)
```

time: 383 us -> 250 us (0.65)
  Pallas kernels: 289 us -> 217 us
  waiting for transfers between devices: 35.4 us -> 2.43 us
  starting transfers between devices: 28.4 us -> 14.9 us
  between operations: 14.3 us -> 0.83 us
    pallas_call x2, Pallas kernels: 264 us -> 172 us  [conv(): pl.pallas_call(functools.partial(conv_kernel, second), grid=(4,), in_spec...]
    all_gather x1 -> x0, waiting for transfers between devices: 30.4 us -> none  [shards(): pool = lax.all_gather(parents, 'tile', axis=0, tiled=True)]
    pallas_call x1, Pallas kernels: 2.59 us -> 23.9 us  [exchange(): pl.pallas_call(exchange_kernel, in_specs=[pl.BlockSpec(memory_space=pl.AN...]
    ppermute x8 -> x4, starting transfers between devices: 28.3 us -> 14.9 us  [shifted(): lax.ppermute(value, axis, [(source, source + steps) for source in range(i...]
  transfers between devices with their start and end apart: 9 -> 4, of which waited for: 2 -> 1; matrix products, arithmetic and copies ran while one was open for 2% -> 2% of each run, Pallas kernels for 35% -> 0%
where the time goes in v1:
time: 250 us; the launch traced here: 248 us
  Pallas kernels  217 us (87%)
  starting transfers between devices  14.9 us (6%)
  other arithmetic  7.95 us (3%)
  local copies, waits for them, and re-layouts  4.64 us (2%)
    pallas_call x2, Pallas kernels, conv(): pl.pallas_call(functools.partial(conv_kernel, second), grid=(4,), in_spec...  172 us
    pallas_call x1, Pallas kernels, exchange(): pl.pallas_call(exchange_kernel, in_specs=[pl.BlockSpec(memory_space=pl.AN...  23.9 us
    pallas_call x1, Pallas kernels, coarse(): pl.pallas_call(coarse_kernel, in_specs=[pl.BlockSpec(memory_space=pltpu.S...  21.2 us
    ppermute x4, starting transfers between devices, shifted(): lax.ppermute(value, axis, [(source, source + steps) for source in range(i...  14.9 us
    select_n x2, other arithmetic, shards(): jnp.where(valid[:, :, None], features[0].reshape(512, 8, 128), 0)  5.94 us
  transfers between devices with their start and end apart: 4, of which 1 were waited for; matrix products, arithmetic and copies ran while one was open for 2% of the time, Pallas kernels for 0%

profile of v1, /device:TPU:120, one launch (start us, length us, event | category | flops | bytes accessed | tf_op | source)
XLA Modules:
  0.0 248.0 jit_solution(1357492852620712872)
XLA Ops:
  0.6 0.0 copy-start
  0.6 0.0 copy-start.1
  0.7 0.9 iota_compare_fusion
  1.6 3.0 %bitcast_select_fusion.1 = bf16[512,8,128]{2,1,0:T(8,128)(2,1)S(1)} fusion(bf16[1,4096,128]{2,1,0:T(8,128)(2,1)} %param.14, pred[512,8]{1,0:T(8,128)(4,1)S(1)} %iota_compare_fusion), kind=kLoop, calls=%fused_computation.1 | loop fusion | flops 524288 | bytes 2101248 | tf_op jit(solution)/shard_map/jit(_where)/select_n | solution.py:304
  4.7 0.0 copy-start.7
  4.7 0.0 copy-start.8
  4.7 1.9 collective-permute-start
  6.6 3.6 %collective-permute-start.1 = (bf16[1024,128]{1,0:T(8,128)(2,1)S(1)}, bf16[1024,128]{1,0:T(8,128)(2,1)S(1)}, u32[]{:S(2)}, u32[]{:S(2)}) collective-permute-start(bf16[1024,128]{1,0:T(8,128)(2,1)S(1)} %get-tuple-element.14), channel_id=1, source_target_pairs={{1,0},{2,1},{3,2},{4,3},{5,4},{6,5},{7,6},{8,7},{9,8},{10,9},{11,1... | collective-permute-start | bytes 786440 | tf_op jit(solution)/shard_map/ppermute | solution.py:21
  10.3 0.2 lt.32
  10.4 0.0 copy-done
  10.5 2.9 %bitcast_select_fusion.mid_ref.rest_0_ = bf16[4096,128]{1,0:T(8,128)(2,1)} fusion(bf16[1,4096,128]{2,1,0:T(8,128)(2,1)S(1)} %copy-done, pred[4096]{0:T(1024)(128)(4,1)S(1)} %lt.32), kind=kLoop, calls=%fused_computation | loop fusion | flops 524288 | bytes 2101248 | tf_op jit(solution)/shard_map/jit(_where)/select_n | solution.py:304
  13.4 0.0 copy-done.1
  13.4 0.3 fusion
  13.7 0.1 copy.20
  13.8 0.0 copy-start.6
  13.8 0.3 copy.30
  14.1 0.8 reshape.91.idx_ref
  14.9 0.0 copy-done.7
  14.9 0.0 copy-done.8
  14.9 0.0 collective-permute-done.lo_ref
  14.9 0.0 copy-start.4
  15.0 0.0 collective-permute-done.1.hi_ref
  15.0 0.0 copy-start.5
  15.0 0.7 copy-done.4
  15.6 0.1 copy-done.5
  15.7 84.7 %conv_first.1.mid_ref = bf16[4096,128]{1,0:T(8,128)(2,1)} custom-call(s32[110592]{0:T(1024)} %reshape.91.idx_ref, s32[512]{0:T(512)} %bitcast.50, bf16[1024,128]{1,0:T(8,128)(2,1)} %copy-done.4, bf16[4096,128]{1,0:T(8,128)(2,1)} %bitcast_select_fusion.mid_ref.rest_0_, bf16[1024,128]{1,0:T(8,128)(2,1)} %copy-done.5, bf16[3456,128]{1,0:T(8,128)(2,1)} %w_in.3, ...), custom_call_target="tpu_custom_call" | custom-call | tf_op jit(solution)/shard_map/conv_first/pallas_call | solution.py:141
  100.4 1.1 fusion.3
  101.5 7.4 %collective-permute-start.2 = (bf16[1024,128]{1,0:T(8,128)(2,1)S(1)}, bf16[1024,128]{1,0:T(8,128)(2,1)S(1)}, u32[]{:S(2)}, u32[]{:S(2)}) collective-permute-start(bf16[1024,128]{1,0:T(8,128)(2,1)S(1)} %get-tuple-element.13), channel_id=1, source_target_pairs={{0,1},{1,2},{2,3},{3,4},{4,5},{5,6},{6,7},{7,8},{8,9},{9,10},{10,1... | collective-permute-start | bytes 786440 | tf_op jit(solution)/shard_map/ppermute | solution.py:21
  108.9 1.9 collective-permute-start.3
  110.8 0.1 fusion.1
  110.9 0.0 copy-done.6
  111.0 0.6 reshape.93.idx_ref
  111.6 0.1 pad_add_fusion
  111.7 0.6 add_add_fusion.codes_ref
  112.3 0.0 collective-permute-done.2.lo_ref
  112.3 0.0 copy-start.2
  112.3 2.4 collective-permute-done.3.hi_ref
  114.7 0.0 copy-start.3
  114.7 0.0 copy-done.2
  114.7 0.7 copy-done.3
  115.4 87.5 %conv_second.1 = (bf16[4096,128]{1,0:T(8,128)(2,1)}, bf16[512,256]{1,0:T(8,128)(2,1)}) custom-call(s32[110592]{0:T(1024)} %reshape.91.idx_ref, s32[512]{0:T(512)} %bitcast.51, bf16[1024,128]{1,0:T(8,128)(2,1)} %copy-done.2, bf16[4096,128]{1,0:T(8,128)(2,1)} %conv_first.1.mid_ref, bf16[1024,128]{1,0:T(8,128)(2,1)} %copy-done.3, bf16[3456,128]{1,0:T(8,128)(2,1)} %w_in.4, ...), custom_call_target="tpu_custom_call" | custom-call | tf_op jit(solution)/shard_map/conv_second/pallas_call | solution.py:141
  202.9 23.9 %exchange.1 = (bf16[4,640,256]{2,1,0:T(8,128)(2,1)}, s32[3,4,8,128]{3,2,1,0:T(8,128)}) custom-call(bf16[512,256]{1,0:T(8,128)(2,1)} %get-tuple-element.7.rows_ref, s32[2,8,128]{2,1,0:T(8,128)} %add_add_fusion.codes_ref), custom_call_target="tpu_custom_call" | custom-call | tf_op jit(solution)/shard_map/exchange/pallas_call | solution.py:204
  226.8 21.2 %coarse.1 = bf16[512,256]{1,0:T(8,128)(2,1)} custom-call(s32[13824]{0:T(1024)} %reshape.93.idx_ref, s32[3,4,8,128]{3,2,1,0:T(8,128)} %get-tuple-element.8.places_ref, bf16[4,640,256]{2,1,0:T(8,128)(2,1)} %get-tuple-element.9.pool_ref, bf16[6912,256]{1,0:T(8,128)(2,1)} %w_in.5, f32[1,256]{1,0:T(1,128)} %bitcast.54), custom_call_target="tpu_custom_call" | custom-call | tf_op jit(solution)/shard_map/coarse/pallas_call | solution.py:265
  (7 shorter events, 0.1 us)
Async XLA Ops:
  0.6 9.8 %copy-start = (bf16[1,4096,128]{2,1,0:T(8,128)(2,1)S(1)}, bf16[1,4096,128]{2,1,0:T(8,128)(2,1)}, u32[]{:S(2)}) copy-start(bf16[1,4096,128]{2,1,0:T(8,128)(2,1)} %param.14) | copy-start | bytes 3145732
  0.6 12.7 %copy-start.1 = (s32[1,4096,27]{1,0,2:T(1,128)S(1)}, s32[1,4096,27]{1,0,2:T(1,128)}, u32[]{:S(2)}) copy-start(s32[1,4096,27]{1,0,2:T(1,128)} %param.15) | copy-start | bytes 1327108
  4.7 10.2 %copy-start.7 = (s32[1,512]{1,0:T(1,128)S(1)}, s32[1,512]{1,0:T(1,128)}, u32[]{:S(2)}) copy-start(s32[1,512]{1,0:T(1,128)} %param.17) | copy-start | bytes 6148
  4.7 10.2 %copy-start.8 = (s32[1,512]{1,0:T(1,128)S(1)}, s32[1,512]{1,0:T(1,128)}, u32[]{:S(2)}) copy-start(s32[1,512]{1,0:T(1,128)} %param.18) | copy-start | bytes 6148
  4.7 10.2 %collective-permute-start = (bf16[1024,128]{1,0:T(8,128)(2,1)S(1)}, bf16[1024,128]{1,0:T(8,128)(2,1)S(1)}, u32[]{:S(2)}, u32[]{:S(2)}) collective-permute-start(bf16[1024,128]{1,0:T(8,128)(2,1)S(1)} %get-tuple-element.15), channel_id=1, source_target_pairs={{0,1},{1,2},{2,3},{3,4},{4,5},{5,6},{6,7},{7,8},{8,9},{9,10},{10,1... | collective-permute-start | bytes 786440 | tf_op jit(solution)/shard_map/ppermute | solution.py:21
  6.6 8.3 %collective-permute-start.1 = (bf16[1024,128]{1,0:T(8,128)(2,1)S(1)}, bf16[1024,128]{1,0:T(8,128)(2,1)S(1)}, u32[]{:S(2)}, u32[]{:S(2)}) collective-permute-start(bf16[1024,128]{1,0:T(8,128)(2,1)S(1)} %get-tuple-element.14), channel_id=1, source_target_pairs={{1,0},{2,1},{3,2},{4,3},{5,4},{6,5},{7,6},{8,7},{9,8},{10,9},{11,1... | collective-permute-start | bytes 786440 | tf_op jit(solution)/shard_map/ppermute | solution.py:21
  13.8 97.1 %copy-start.6 = (s32[1,512,27]{1,0,2:T(1,128)S(1)}, s32[1,512,27]{1,0,2:T(1,128)}, u32[]{:S(2)}) copy-start(s32[1,512,27]{1,0,2:T(1,128)} %param.19) | copy-start | bytes 165892
  14.9 0.7 copy-start.4
  15.0 0.8 copy-start.5
  101.5 10.8 %collective-permute-start.2 = (bf16[1024,128]{1,0:T(8,128)(2,1)S(1)}, bf16[1024,128]{1,0:T(8,128)(2,1)S(1)}, u32[]{:S(2)}, u32[]{:S(2)}) collective-permute-start(bf16[1024,128]{1,0:T(8,128)(2,1)S(1)} %get-tuple-element.13), channel_id=1, source_target_pairs={{0,1},{1,2},{2,3},{3,4},{4,5},{5,6},{6,7},{7,8},{8,9},{9,10},{10,1... | collective-permute-start | bytes 786440 | tf_op jit(solution)/shard_map/ppermute | solution.py:21
  108.9 5.8 %collective-permute-start.3 = (bf16[1024,128]{1,0:T(8,128)(2,1)S(1)}, bf16[1024,128]{1,0:T(8,128)(2,1)S(1)}, u32[]{:S(2)}, u32[]{:S(2)}) collective-permute-start(bf16[1024,128]{1,0:T(8,128)(2,1)S(1)} %get-tuple-element.12), channel_id=1, source_target_pairs={{1,0},{2,1},{3,2},{4,3},{5,4},{6,5},{7,6},{8,7},{9,8},{10,9},{11,1... | collective-permute-start | bytes 786440 | tf_op jit(solution)/shard_map/ppermute | solution.py:21
  112.3 2.4 copy-start.2
  114.7 0.7 copy-start.3

commit v2 on v1

--- a/solution.py
+++ b/solution.py
@@ -69,7 +69,7 @@
     *rest,
 ):
     if second:
-        x_ref, wd_ref, gain_down_ref, out_ref, down_ref, table, gathered, acc_ref, fine_ref = rest
+        x_ref, wd_ref, gain_down_ref, place_ref, out_ref, down_ref, edge_ref, table, gathered, acc_ref, fine_ref, raw, placed = rest
     else:
         out_ref, table, gathered, acc_ref = rest
     step = pl.program_id(0)
@@ -80,7 +80,20 @@
     def _():
         table[:PAD, :] = jnp.zeros((PAD, 128), jnp.float32)
         table[pl.ds(PAD, 1024), :] = lo_ref[...].astype(jnp.float32)
-        table[pl.ds(PAD + 1024, 4096), :] = mid_ref[...].astype(jnp.float32)
+        if second:
+            table[pl.ds(PAD + 1024, 4096), :] = mid_ref[...].astype(jnp.float32)
+        else:
+
+            def masked(g, _):
+                for i in range(8):
+                    block = g * 16 + 2 * i
+                    row = pl.multiple_of(block * 8, 16)
+                    valid = jnp.concatenate([sub16 < counts_ref[block], sub16 < counts_ref[block + 1]], 0)
+                    value = jnp.where(valid, mid_ref[pl.ds(row, 16), :].astype(jnp.float32), 0.0)
+                    table[pl.ds(pl.multiple_of(row + (PAD + 1024), 8), 16), :] = value
+                return 0
+
+            lax.fori_loop(0, 32, masked, 0)
         table[pl.ds(PAD + 5120, 1024), :] = hi_ref[...].astype(jnp.float32)
 
     gather_rows(idx_ref, ((table, 0),), gathered, 8, masks)
@@ -114,21 +127,41 @@
                     child = fine_ref[pl.ds(c * 512 + j, 64, stride=8), :].astype(jnp.bfloat16)
                     total += jnp.dot(child, wd_ref[j * 128 : (j + 1) * 128, :], preferred_element_type=jnp.float32)
                 value = jnp.maximum(normed(total, gain_down_ref[...]), 0.0)
-                down_ref[pl.ds(pl.multiple_of(c * 64, 64), 64), :] = value.astype(jnp.bfloat16)
+                row = pl.multiple_of(c * 64, 64)
+                raw[pl.ds(row, 64), :] = value[:, :128]
+                raw[pl.ds(row + 512, 64), :] = value[:, 128:]
                 return 0
 
             lax.fori_loop(0, 8, down, 0)
+            for n, row in enumerate((0, 448)):
+                for h in range(2):
+                    edge_ref[n * 64 : n * 64 + 64, h * 128 : h * 128 + 128] = raw[
+                        h * 512 + row : h * 512 + row + 64, :
+                    ].astype(jnp.bfloat16)
+            placed[...] = jnp.zeros_like(placed)
+
+            def put(g, _):
+                for i in range(16):
+                    at = place_ref[g * 16 + i]
+                    placed[pl.ds(at, 1), :] = raw[pl.ds(g * 16 + i, 1), :]
+                    placed[pl.ds(at + 520, 1), :] = raw[pl.ds(g * 16 + i + 512, 1), :]
+                return 0
+
+            lax.fori_loop(0, 32, put, 0)
+            down_ref[:, :128] = placed[:512, :].astype(jnp.bfloat16)
+            down_ref[:, 128:] = placed[520:1032, :].astype(jnp.bfloat16)
 
 
 def whole(shape):
     return pl.BlockSpec(shape, lambda i: (0,) * len(shape))
 
 
-def conv(second, idx, counts, lo, mid, hi, w, gain, *more):
+def conv(second, idx, counts, lo, mid, hi, w, gain, *more, places=()):
     specs = [
         pl.BlockSpec((8 * K * TILE,), lambda i: (i,), memory_space=pltpu.SMEM),
         pl.BlockSpec(memory_space=pltpu.SMEM),
     ] + [whole(a.shape) for a in (lo, mid, hi, w, gain) + more]
+    specs += [pl.BlockSpec(memory_space=pltpu.SMEM) for _ in places]
     out_shape = [jax.ShapeDtypeStruct((4096, 128), jnp.bfloat16)]
     scratch = [
         pltpu.VMEM((PAD + 6144 + 8, 128), jnp.float32),
@@ -137,7 +170,10 @@
     ]
     if second:
         out_shape.append(jax.ShapeDtypeStruct((512, 256), jnp.bfloat16))
+        out_shape.append(jax.ShapeDtypeStruct((128, 256), jnp.bfloat16))
         scratch.append(pltpu.VMEM((4096, 128), jnp.float32))
+        scratch.append(pltpu.VMEM((1024, 128), jnp.float32))
+        scratch.append(pltpu.VMEM((1040, 128), jnp.float32))
     return pl.pallas_call(
         functools.partial(conv_kernel, second),
         grid=(4,),
@@ -147,7 +183,7 @@
         scratch_shapes=scratch,
         name="conv_second" if second else "conv_first",
         compiler_params=pltpu.CompilerParams(vmem_limit_bytes=VMEM_LIMIT),
-    )(idx, counts, lo, mid, hi, w, gain, *more)
+    )(idx, counts, lo, mid, hi, w, gain, *more, *places)
 
 
 HALF = 2048 + 16
@@ -155,22 +191,24 @@
 REACH = 640
 
 
-def exchange_kernel(rows_ref, codes_ref, pool_ref, places_ref, send_sem, recv_sem, local_sem):
-    tile, me = lax.axis_index("tile"), lax.axis_index("morton")
-    tiles, ranges = lax.axis_size("tile"), lax.axis_size("morton")
-    above, below = lax.rem(me + 1, ranges), lax.rem(me + ranges - 1, ranges)
-    peers = [lax.rem(tile + d, tiles) for d in range(tiles)]
-
+def ring(axis):
+    me, count = lax.axis_index(axis), lax.axis_size(axis)
+    return lax.rem(me + 1, count), lax.rem(me + count - 1, count)
+
+
+def greet(partners):
     barrier = pltpu.get_barrier_semaphore()
-    partners = [(peers[d], me) for d in range(1, tiles)] + [(peers[d], m) for m in (above, below) for d in range(tiles)]
     for partner in partners:
         pl.semaphore_signal(barrier, inc=1, device_id=partner, device_id_type=pl.DeviceIdType.MESH)
     pl.semaphore_wait(barrier, len(partners))
 
-    copies = []
+
+def sender(send_sem, recv_sem):
+    count = [0]
 
     def send(src, dst, partner):
-        n = len(copies)
+        n = count[0]
+        count[0] += 1
         copy = pltpu.make_async_remote_copy(
             src_ref=src,
             dst_ref=dst,
@@ -180,43 +218,91 @@
             device_id_type=pl.DeviceIdType.MESH,
         )
         copy.start()
-        copies.append(copy)
-
-    for d in (2, 1, 3):
-        send(rows_ref, pool_ref.at[tile, pl.ds(0, 512)], (peers[d], me))
-        send(codes_ref.at[0], places_ref.at[0, tile], (peers[d], me))
-    for d in range(tiles):
-        send(rows_ref.at[pl.ds(448, 64)], pool_ref.at[tile, pl.ds(512, 64)], (peers[d], above))
-        send(codes_ref.at[1], places_ref.at[1, tile], (peers[d], above))
-        send(rows_ref.at[pl.ds(0, 64)], pool_ref.at[tile, pl.ds(576, 64)], (peers[d], below))
-        send(codes_ref.at[1], places_ref.at[2, tile], (peers[d], below))
-    own = [
-        pltpu.make_async_copy(rows_ref, pool_ref.at[tile, pl.ds(0, 512)], local_sem.at[0]),
-        pltpu.make_async_copy(codes_ref.at[0], places_ref.at[0, tile], local_sem.at[1]),
+        return copy
+
+    return send
+
+
+def halo_kernel(field_ref, lo_ref, hi_ref, send_sem, recv_sem):
+    tile = lax.axis_index("tile")
+    above, below = ring("morton")
+    greet([(tile, above), (tile, below)])
+    send = sender(send_sem, recv_sem)
+    copies = [
+        send(field_ref.at[pl.ds(3072, 1024)], lo_ref, (tile, above)),
+        send(field_ref.at[pl.ds(0, 1024)], hi_ref, (tile, below)),
     ]
-    for copy in own:
-        copy.start()
-    for copy in own + copies:
+    for copy in copies:
         copy.wait()
 
 
-def exchange(rows, codes):
+def halo_of(field):
+    return pl.pallas_call(
+        halo_kernel,
+        in_specs=[pl.BlockSpec(memory_space=pl.ANY)],
+        out_specs=[pl.BlockSpec(memory_space=pl.ANY)] * 2,
+        out_shape=[jax.ShapeDtypeStruct((1024, 128), jnp.bfloat16)] * 2,
+        scratch_shapes=[pltpu.SemaphoreType.DMA((2,)), pltpu.SemaphoreType.DMA((2,))],
+        name="halo",
+        compiler_params=pltpu.CompilerParams(collective_id=1, has_side_effects=True),
+    )(field)
+
+
+def exchange_kernel(rows_ref, edge_ref, codes_ref, pool_ref, places_ref, send_sem, recv_sem, local_sem):
+    tile, me = lax.axis_index("tile"), lax.axis_index("morton")
+    right, left = ring("tile")
+    above, below = ring("morton")
+    opposite = lax.rem(tile + 2, lax.axis_size("tile"))
+    tiles = (tile, right, left, opposite)
+    greet([(right, me), (left, me)] + [(t, m) for t in tiles for m in (above, below)])
+
+    send = sender(send_sem, recv_sem)
+    first, last = pl.ds(0, 256), pl.ds(256, 256)
+    from_below, from_above = pl.ds(512, 64), pl.ds(576, 64)
+    right_first = send(rows_ref.at[first], pool_ref.at[tile, first], (right, me))
+    left_last = send(rows_ref.at[last], pool_ref.at[tile, last], (left, me))
+    handed = {}
+    for n, t in enumerate((right, left, tile)):
+        handed[n, 0] = send(edge_ref.at[pl.ds(64, 64)], pool_ref.at[tile, from_below], (t, above))
+        handed[n, 1] = send(edge_ref.at[pl.ds(0, 64)], pool_ref.at[tile, from_above], (t, below))
+    others = [send(rows_ref.at[last], pool_ref.at[tile, last], (right, me))]
+    others.append(send(rows_ref.at[first], pool_ref.at[tile, first], (left, me)))
+    for t in tiles:
+        others.append(send(codes_ref, places_ref.at[0, tile], (t, above)))
+        others.append(send(codes_ref, places_ref.at[1, tile], (t, below)))
+    own = pltpu.make_async_copy(rows_ref, pool_ref.at[tile, pl.ds(0, 512)], local_sem)
+    own.start()
+
+    relays = ((right_first, left, first, right), (left_last, right, last, left))
+    relays += ((handed[0, 0], left, from_below, right), (handed[1, 1], right, from_above, left))
+    passed = []
+    for copy, source, part, target in relays:
+        copy.wait_recv()
+        passed.append(send(pool_ref.at[source, part], pool_ref.at[source, part], (target, me)))
+    for copy, _, _, _ in relays:
+        copy.wait_send()
+    own.wait()
+    for copy in [handed[0, 1], handed[1, 0], handed[2, 0], handed[2, 1]] + others + passed:
+        copy.wait()
+
+
+def exchange(rows, edges, codes):
     return pl.pallas_call(
         exchange_kernel,
-        in_specs=[pl.BlockSpec(memory_space=pl.ANY)] * 2,
+        in_specs=[pl.BlockSpec(memory_space=pl.ANY)] * 3,
         out_specs=[pl.BlockSpec(memory_space=pl.ANY)] * 2,
         out_shape=[
             jax.ShapeDtypeStruct((4, REACH, 256), jnp.bfloat16),
-            jax.ShapeDtypeStruct((3, 4, 8, 128), jnp.int32),
+            jax.ShapeDtypeStruct((2, 4, 8, 128), jnp.int32),
         ],
         scratch_shapes=[
             pltpu.SemaphoreType.DMA((22,)),
             pltpu.SemaphoreType.DMA((22,)),
-            pltpu.SemaphoreType.DMA((2,)),
+            pltpu.SemaphoreType.DMA,
         ],
         name="exchange",
         compiler_params=pltpu.CompilerParams(collective_id=0, has_side_effects=True),
-    )(rows, codes)
+    )(rows, edges, codes)
 
 
 def coarse_kernel(idx_ref, places_ref, pool_ref, w_in, gain_ref, out_ref, table, source, gathered, acc_ref):
@@ -225,26 +311,25 @@
     table[HALF : HALF + PAD, :] = jnp.zeros((PAD, 128), jnp.float32)
 
     def tile_rows(t, _):
-        source[:REACH, :] = pool_ref[t, :, :128].astype(jnp.float32)
-        source[REACH:, :] = pool_ref[t, :, 128:].astype(jnp.float32)
-
-        def put(kind, line, col, row):
-            for i in range(16):
-                at = places_ref[kind, t, line, col + i]
-                table[pl.ds(at, 1), :] = source[pl.ds(row + i, 1), :]
-                table[pl.ds(at + HALF, 1), :] = source[pl.ds(row + i + REACH, 1), :]
-
-        def own(g, _):
-            put(0, g // 8, (g % 8) * 16, pl.multiple_of(g * 16, 16))
-            return 0
-
-        lax.fori_loop(0, 32, own, 0)
-        for g in range(4):
-            put(1, 0, g * 16, 512 + g * 16)
-            put(2, 0, 64 + g * 16, 576 + g * 16)
+        row = pl.multiple_of(PAD + t * 512, 8)
+        for h in range(2):
+            cols = slice(h * 128, h * 128 + 128)
+            table[pl.ds(row + h * HALF, 512), :] = pool_ref[t, :512, cols].astype(jnp.float32)
+            source[pl.ds((t * 2 + h) * 128, 128), :] = pool_ref[t, 512:, cols].astype(jnp.float32)
         return 0
 
     lax.fori_loop(0, 4, tile_rows, 0)
+
+    def handed(t, _):
+        for kind in range(2):
+            for i in range(64):
+                at = places_ref[kind, t, 0, kind * 64 + i]
+                row = t * 256 + kind * 64 + i
+                table[pl.ds(at, 1), :] = source[pl.ds(row, 1), :]
+                table[pl.ds(at + HALF, 1), :] = source[pl.ds(row + 128, 1), :]
+        return 0
+
+    lax.fori_loop(0, 4, handed, 0)
     gather_rows(idx_ref, ((table, 0), (table, HALF)), gathered, 4, masks)
     acc_ref[...] = jnp.dot(gathered[...], w_in[...], preferred_element_type=jnp.float32)
     first = PAD + 512 * lax.axis_index("tile")
@@ -269,7 +354,7 @@
         out_shape=jax.ShapeDtypeStruct((512, 256), jnp.bfloat16),
         scratch_shapes=[
             pltpu.VMEM((2 * HALF, 128), jnp.float32),
-            pltpu.VMEM((2 * REACH, 128), jnp.float32),
+            pltpu.VMEM((1024, 128), jnp.float32),
             pltpu.VMEM((512, K * 256), jnp.bfloat16),
             pltpu.VMEM((512, 256), jnp.float32),
         ],
@@ -300,8 +385,13 @@
     gain_coarse,
 ):
     lane_ids = jnp.arange(8, dtype=jnp.int32)
-    valid = lane_ids[None, :] < counts[0][:, None]
-    field = jnp.where(valid[:, :, None], features[0].reshape(512, 8, 128), 0).astype(jnp.bfloat16).reshape(4096, 128)
+
+    def masked(first):
+        valid = lane_ids[None, :] < counts[0, first : first + 128, None]
+        rows = features[0, 8 * first : 8 * first + 1024].reshape(128, 8, 128)
+        return jnp.where(valid[:, :, None], rows, 0).astype(jnp.bfloat16).reshape(1024, 128)
+
+    lo, hi = shifted(masked(384), "morton", 1), shifted(masked(0), "morton", -1)
     by_offset = neighbours[0].T
     local = by_offset + jnp.arange(4096, dtype=jnp.int32)[None, :]
     idx = by_tiles(jnp.where(by_offset < 0, -1, local))
@@ -315,19 +405,15 @@
         return jnp.where(destination == to, at, NOWHERE)
 
     edges = jnp.concatenate([handed(me + 1)[448:], handed(me - 1)[:64]])
-    codes = jnp.stack([handed(me).reshape(4, 128), jnp.broadcast_to(edges[None], (4, 128))])
-    codes = jnp.concatenate([codes, codes], axis=1)
-
-    def halo(v):
-        return shifted(v[3072:], "morton", 1), shifted(v[:1024], "morton", -1)
-
-    lo, hi = halo(field)
-    (act,) = conv(False, idx, counts[0], lo, field, hi, w_first, gain_first[None])
-    lo, hi = halo(act)
-    fine, rows = conv(
-        True, idx, counts[0], lo, act, hi, w_second, gain_second[None], field, w_down, gain_down[None]
+    codes = jnp.broadcast_to(edges[None], (8, 128))
+    kept = jnp.where(destination == me, slot[0], 512)
+
+    (act,) = conv(False, idx, counts[0], lo, features[0], hi, w_first, gain_first[None])
+    lo, hi = halo_of(act)
+    fine, rows, edge_rows = conv(
+        True, idx, counts[0], lo, act, hi, w_second, gain_second[None], features[0], w_down, gain_down[None], places=(kept,)
     )
-    pool, places = exchange(rows, codes)
+    pool, places = exchange(rows, edge_rows, codes)
     out = coarse(coarse_idx, places, pool, w_coarse, gain_coarse[None])
     return fine[None], out[None]
 

time: 250 us -> 234 us (0.936)
  starting transfers between devices: 14.9 us -> 5.56 us
  other arithmetic: 7.95 us -> 3.55 us
  Pallas kernels: 217 us -> 220 us
    pallas_call x0 -> x1, Pallas kernels: none -> 10.4 us  [halo_of(): pl.pallas_call(halo_kernel, in_specs=[pl.BlockSpec(memory_space=pl.ANY)],...]
    ppermute x4 -> x2, starting transfers between devices: 14.9 us -> 5.56 us  [shifted(): lax.ppermute(value, axis, [(source, source + steps) for source in range(i...]
    pallas_call x1, Pallas kernels: 21.2 us -> 14.8 us  [coarse(): pl.pallas_call(coarse_kernel, in_specs=[pl.BlockSpec(memory_space=pltpu.S...]
    select_n x3 -> x1, other arithmetic: 5.95 us -> 1.37 us  [masked(): jnp.where(valid[:, :, None], rows, 0).astype(jnp.bfloat16)]
    pallas_call x1, Pallas kernels: 23.9 us -> 20.9 us  [exchange(): pl.pallas_call(exchange_kernel, in_specs=[pl.BlockSpec(memory_space=pl.AN...]
  transfers between devices with their start and end apart: 4 -> 2, of which waited for: 1 -> 0; matrix products, arithmetic and copies ran while one was open for 2% -> 2% of each run, Pallas kernels for 0% -> 0%
where the time goes in v2:
time: 234 us
  Pallas kernels  220 us (94%)
  starting transfers between devices  5.56 us (2%)
  local copies, waits for them, and re-layouts  4.15 us (2%)
  other arithmetic  3.55 us (2%)
    pallas_call x2, Pallas kernels, conv(): pl.pallas_call(functools.partial(conv_kernel, second), grid=(4,), in_spec...  174 us
    pallas_call x1, Pallas kernels, exchange(): pl.pallas_call(exchange_kernel, in_specs=[pl.BlockSpec(memory_space=pl.AN...  20.9 us
    pallas_call x1, Pallas kernels, coarse(): pl.pallas_call(coarse_kernel, in_specs=[pl.BlockSpec(memory_space=pltpu.S...  14.8 us
    pallas_call x1, Pallas kernels, halo_of(): pl.pallas_call(halo_kernel, in_specs=[pl.BlockSpec(memory_space=pl.ANY)],...  10.4 us
    ppermute x2, starting transfers between devices, shifted(): lax.ppermute(value, axis, [(source, source + steps) for source in range(i...  5.56 us
  transfers between devices with their start and end apart: 2, of which 0 were waited for; matrix products, arithmetic and copies ran while one was open for 2% of the time, Pallas kernels for 0%

profile of v2, /device:TPU:120, one launch (start us, length us, event | category | flops | bytes accessed | tf_op | source)
XLA Modules:
  0.0 233.7 jit_solution(585279746487411578)
XLA Ops:
  0.6 0.0 copy-start.2
  0.6 0.0 copy-start.3
  0.7 0.0 copy-start.4
  0.7 0.7 slice_bitcast_fusion
  1.4 0.1 iota_compare_fusion
  1.5 0.1 lt.56
  1.6 0.1 lt.61
  1.7 1.4 bitcast_select_fusion
  3.0 1.9 collective-permute-start
  5.0 3.6 %collective-permute-start.1 = (bf16[1024,128]{1,0:T(8,128)(2,1)S(1)}, bf16[1024,128]{1,0:T(8,128)(2,1)S(1)}, u32[]{:S(2)}, u32[]{:S(2)}) collective-permute-start(bf16[1024,128]{1,0:T(8,128)(2,1)S(1)} %get-tuple-element.16), channel_id=1, source_target_pairs={{1,0},{2,1},{3,2},{4,3},{5,4},{6,5},{7,6},{8,7},{9,8},{10,9},{11,1... | collective-permute-start | bytes 786440 | tf_op jit(solution)/shard_map/ppermute | solution.py:21
  8.6 1.3 fusion
  10.0 0.1 copy.20
  10.1 0.3 copy.30
  10.4 0.8 reshape.82.idx_ref
  11.2 0.0 copy-done.2
  11.3 0.6 reshape.84.idx_ref
  11.9 0.0 copy-done.3
  11.9 0.0 copy-done.4
  11.9 0.6 broadcast_add_fusion
  12.5 0.1 fusion.1
  12.5 0.1 pad_add_fusion
  12.6 0.0 collective-permute-done.lo_ref
  12.6 0.0 copy-start
  12.6 0.0 collective-permute-done.1.hi_ref
  12.6 0.0 copy-start.1
  12.7 0.7 copy-done
  13.3 0.1 copy-done.1
  13.4 85.2 %conv_first.1.field_ref.mid_ref = bf16[4096,128]{1,0:T(8,128)(2,1)} custom-call(s32[110592]{0:T(1024)} %reshape.82.idx_ref, s32[512]{0:T(512)} %bitcast.52, bf16[1024,128]{1,0:T(8,128)(2,1)} %copy-done, bf16[4096,128]{1,0:T(8,128)(2,1)} %bitcast.44, bf16[1024,128]{1,0:T(8,128)(2,1)} %copy-done.1, bf16[3456,128]{1,0:T(8,128)(2,1)} %w_in.3, f32[1,128]{1,0:T(1,128)} %bitcast.58), custom_call_target="tpu_custom_call" | custom-call | tf_op jit(solution)/shard_map/conv_first/pallas_call | solution.py:177
  98.7 10.4 %halo.1 = (bf16[1024,128]{1,0:T(8,128)(2,1)}, bf16[1024,128]{1,0:T(8,128)(2,1)}) custom-call(bf16[4096,128]{1,0:T(8,128)(2,1)} %conv_first.1.field_ref.mid_ref), custom_call_target="tpu_custom_call" | custom-call | tf_op jit(solution)/shard_map/halo/pallas_call | solution.py:240
  109.1 88.3 %conv_second.1 = (bf16[4096,128]{1,0:T(8,128)(2,1)}, bf16[512,256]{1,0:T(8,128)(2,1)}, bf16[128,256]{1,0:T(8,128)(2,1)}) custom-call(s32[110592]{0:T(1024)} %reshape.82.idx_ref, s32[512]{0:T(512)} %bitcast.53, bf16[1024,128]{1,0:T(8,128)(2,1)} %get-tuple-element.9.lo_ref, bf16[4096,128]{1,0:T(8,128)(2,1)} %conv_first.1.field_ref.mid_ref, ...), custom_call_target="tpu_custom_call" | custom-call | tf_op jit(solution)/shard_map/conv_second/pallas_call | solution.py:177
  197.4 0.6 broadcast_in_dim.69.codes_ref
  198.0 20.9 %exchange.1 = (bf16[4,640,256]{2,1,0:T(8,128)(2,1)}, s32[2,4,8,128]{3,2,1,0:T(8,128)}) custom-call(bf16[512,256]{1,0:T(8,128)(2,1)} %get-tuple-element.12.rows_ref, bf16[128,256]{1,0:T(8,128)(2,1)} %get-tuple-element.13.edge_ref, s32[8,128]{1,0:T(8,128)} %broadcast_in_dim.69.codes_ref), custom_call_target="tpu_custom_call" | custom-call | tf_op jit(solution)/shard_map/exchange/pallas_call | solution.py:290
  218.9 14.8 %coarse.1 = bf16[512,256]{1,0:T(8,128)(2,1)} custom-call(s32[13824]{0:T(1024)} %reshape.84.idx_ref, s32[2,4,8,128]{3,2,1,0:T(8,128)} %get-tuple-element.14.places_ref, bf16[4,640,256]{2,1,0:T(8,128)(2,1)} %get-tuple-element.15.pool_ref, bf16[6912,256]{1,0:T(8,128)(2,1)} %w_in.5, f32[1,256]{1,0:T(1,128)} %bitcast.56), custom_call_target="tpu_custom_call" | custom-call | tf_op jit(solution)/shard_map/coarse/pallas_call | solution.py:350
  (4 shorter events, 0.1 us)
Async XLA Ops:
  0.6 10.6 %copy-start.2 = (s32[1,512,27]{1,0,2:T(1,128)S(1)}, s32[1,512,27]{1,0,2:T(1,128)}, u32[]{:S(2)}) copy-start(s32[1,512,27]{1,0,2:T(1,128)} %param.19) | copy-start | bytes 165892
  0.6 11.2 %copy-start.3 = (s32[1,512]{1,0:T(1,128)S(1)}, s32[1,512]{1,0:T(1,128)}, u32[]{:S(2)}) copy-start(s32[1,512]{1,0:T(1,128)} %param.17) | copy-start | bytes 6148
  0.7 11.2 %copy-start.4 = (s32[1,512]{1,0:T(1,128)S(1)}, s32[1,512]{1,0:T(1,128)}, u32[]{:S(2)}) copy-start(s32[1,512]{1,0:T(1,128)} %param.18) | copy-start | bytes 6148
  3.0 9.6 %collective-permute-start = (bf16[1024,128]{1,0:T(8,128)(2,1)S(1)}, bf16[1024,128]{1,0:T(8,128)(2,1)S(1)}, u32[]{:S(2)}, u32[]{:S(2)}) collective-permute-start(bf16[1024,128]{1,0:T(8,128)(2,1)S(1)} %get-tuple-element.17), channel_id=1, source_target_pairs={{0,1},{1,2},{2,3},{3,4},{4,5},{5,6},{6,7},{7,8},{8,9},{9,10},{10,1... | collective-permute-start | bytes 786440 | tf_op jit(solution)/shard_map/ppermute | solution.py:21
  5.0 7.7 %collective-permute-start.1 = (bf16[1024,128]{1,0:T(8,128)(2,1)S(1)}, bf16[1024,128]{1,0:T(8,128)(2,1)S(1)}, u32[]{:S(2)}, u32[]{:S(2)}) collective-permute-start(bf16[1024,128]{1,0:T(8,128)(2,1)S(1)} %get-tuple-element.16), channel_id=1, source_target_pairs={{1,0},{2,1},{3,2},{4,3},{5,4},{6,5},{7,6},{8,7},{9,8},{10,9},{11,1... | collective-permute-start | bytes 786440 | tf_op jit(solution)/shard_map/ppermute | solution.py:21
  12.6 0.7 copy-start
  12.6 0.8 copy-start.1

commit v3 on v2

--- a/solution.py
+++ b/solution.py
@@ -11,6 +11,9 @@
 TILE = 128
 GROUPS = TILE // 16
 PAD = 8
+PLAN = 1280
+LISTED = 1056
+MOSTLY = 640
 EPS = 1e-05
 VMEM_LIMIT = 58 * 2**20
 
@@ -29,28 +32,54 @@
 def gather_rows(idx_ref, tables, dst_ref, tiles, masks):
     width = 128 * len(tables)
 
+    def body(step, _):
+        for part in range(2):
+            g = step * 2 + part
+            base_ref = idx_ref.at[pl.ds((step // 4) * (K * TILE) + (step % 4) * 32, (K - 1) * TILE + 32)]
+            for k in range(K):
+                both = [[] for _ in tables]
+                for h in range(2):
+                    first = k * TILE + part * 16 + h * 8
+                    lead = 8 if first else 0
+                    at = base_ref.at[pl.ds(first - lead, 8 + lead)]
+                    acc = [None for _ in tables]
+                    for i in range(8):
+                        row = at[lead + i]
+                        for n, (table, base) in enumerate(tables):
+                            v = table[pl.ds(row + (base + PAD - i), 8), :]
+                            acc[n] = v if i == 0 else jnp.where(masks[i], v, acc[n])
+                    for n in range(len(tables)):
+                        both[n].append(acc[n])
+                for n in range(len(tables)):
+                    col = k * width + n * 128
+                    dst_ref[pl.ds(pl.multiple_of(g * 16, 16), 16), col : col + 128] = jnp.concatenate(
+                        both[n], 0
+                    ).astype(jnp.bfloat16)
+        return 0
+
+    lax.fori_loop(0, tiles * 4, body, 0)
+
+
+def gather_listed(idx_ref, plan_ref, first, groups, table, dst_ref, masks):
     def body(g, _):
-        base_ref = idx_ref.at[pl.ds((g // GROUPS) * (K * TILE) + (g % GROUPS) * 16, (K - 1) * TILE + 16)]
-        for k in range(K):
-            both = [[] for _ in tables]
-            for h in range(2):
-                at = base_ref.at[pl.ds(k * TILE + h * 8, 8)]
-                acc = [None for _ in tables]
+        both = []
+        for h in range(2):
+            listed = plan_ref.at[pl.ds(first + g * 16 + h * 8, 8)]
+            at = [idx_ref.at[pl.ds(listed[i], (K - 1) * TILE + 1)] for i in range(8)]
+            both.append([])
+            for k in range(K):
+                acc = None
                 for i in range(8):
-                    row = at[i]
-                    for n, (table, base) in enumerate(tables):
-                        v = table[pl.ds(row + (base + PAD - i), 8), :]
-                        acc[n] = v if i == 0 else jnp.where(masks[i], v, acc[n])
-                for n in range(len(tables)):
-                    both[n].append(acc[n])
-            for n in range(len(tables)):
-                col = k * width + n * 128
-                dst_ref[pl.ds(pl.multiple_of(g * 16, 16), 16), col : col + 128] = jnp.concatenate(
-                    both[n], 0
-                ).astype(jnp.bfloat16)
-        return 0
-
-    lax.fori_loop(0, tiles * GROUPS, body, 0)
+                    v = table[pl.ds(at[i][k * TILE] + (PAD - i), 8), :]
+                    acc = v if i == 0 else jnp.where(masks[i], v, acc)
+                both[h].append(acc)
+                if h:
+                    dst_ref[pl.ds(pl.multiple_of(g * 16, 16), 16), k * 128 : k * 128 + 128] = jnp.concatenate(
+                        [both[0][k], acc], 0
+                    ).astype(jnp.bfloat16)
+        return 0
+
+    lax.fori_loop(0, groups, body, 0)
 
 
 def normed(h, gain):
@@ -60,6 +89,7 @@
 def conv_kernel(
     second,
     idx_ref,
+    plan_ref,
     counts_ref,
     lo_ref,
     mid_ref,
@@ -96,13 +126,20 @@
             lax.fori_loop(0, 32, masked, 0)
         table[pl.ds(PAD + 5120, 1024), :] = hi_ref[...].astype(jnp.float32)
 
-    gather_rows(idx_ref, ((table, 0),), gathered, 8, masks)
-    acc_ref[...] = jnp.dot(gathered[...], w_in[...], preferred_element_type=jnp.float32)
+    plan = step * PLAN
+    total = plan_ref[plan + LISTED + 128]
+    gather_listed(idx_ref, plan_ref, plan, (total + 15) // 16, table, gathered, masks)
+    acc_ref[:MOSTLY, :] = jnp.dot(gathered[:MOSTLY, :], w_in[...], preferred_element_type=jnp.float32)
+
+    @pl.when(total > MOSTLY)
+    def _():
+        acc_ref[MOSTLY:1024, :] = jnp.dot(gathered[MOSTLY:, :], w_in[...], preferred_element_type=jnp.float32)
 
     def epilogue(tile, _):
         gain = gain_ref[...]
         for i in range(GROUPS):
-            h = normed(acc_ref[pl.ds(pl.multiple_of(tile * TILE + i * 16, 16), 16), :], gain)
+            start = plan_ref.at[pl.ds(plan + LISTED + tile * GROUPS * 2 + 2 * i, 2)]
+            h = normed(jnp.concatenate([acc_ref[pl.ds(start[0], 8), :], acc_ref[pl.ds(start[1], 8), :]], 0), gain)
             row = pl.multiple_of(step * 1024 + tile * TILE + i * 16, 16)
             if second:
                 h = x_ref[pl.ds(row, 16), :].astype(jnp.float32) + h
@@ -156,9 +193,10 @@
     return pl.BlockSpec(shape, lambda i: (0,) * len(shape))
 
 
-def conv(second, idx, counts, lo, mid, hi, w, gain, *more, places=()):
+def conv(second, idx, plan, counts, lo, mid, hi, w, gain, *more, places=()):
     specs = [
         pl.BlockSpec((8 * K * TILE,), lambda i: (i,), memory_space=pltpu.SMEM),
+        pl.BlockSpec(memory_space=pltpu.SMEM),
         pl.BlockSpec(memory_space=pltpu.SMEM),
     ] + [whole(a.shape) for a in (lo, mid, hi, w, gain) + more]
     specs += [pl.BlockSpec(memory_space=pltpu.SMEM) for _ in places]
@@ -166,7 +204,7 @@
     scratch = [
         pltpu.VMEM((PAD + 6144 + 8, 128), jnp.float32),
         pltpu.VMEM((1024, K * 128), jnp.bfloat16),
-        pltpu.VMEM((1024, 128), jnp.float32),
+        pltpu.VMEM((1024 + 8, 128), jnp.float32),
     ]
     if second:
         out_shape.append(jax.ShapeDtypeStruct((512, 256), jnp.bfloat16))
@@ -183,7 +221,7 @@
         scratch_shapes=scratch,
         name="conv_second" if second else "conv_first",
         compiler_params=pltpu.CompilerParams(vmem_limit_bytes=VMEM_LIMIT),
-    )(idx, counts, lo, mid, hi, w, gain, *more, *places)
+    )(idx, plan, counts, lo, mid, hi, w, gain, *more, *places)
 
 
 HALF = 2048 + 16
@@ -368,6 +406,20 @@
     return index.reshape(K, rows // TILE, TILE).transpose(1, 0, 2).reshape(-1)
 
 
+def plan_of(counts):
+    held = counts.reshape(4, 128)
+    block = jnp.arange(128, dtype=jnp.int32)
+    ends = jnp.sum(jnp.where(block[None, :] <= block[:, None], held[:, None, :], 0), axis=-1)
+    place = jnp.arange(LISTED, dtype=jnp.int32)
+    past = ends[:, None, :] <= place[None, :, None]
+    at = jnp.sum(past.astype(jnp.int32), axis=-1)
+    start = jnp.max(jnp.where(past, ends[:, None, :], 0), axis=-1)
+    entry = (at // 16) * (K * TILE) + (at % 16) * 8 + place[None, :] - start
+    listed = jnp.where(at < 128, entry, 0)
+    rest = jnp.broadcast_to(ends[:, 127:], (4, PLAN - LISTED - 128))
+    return jnp.concatenate([listed, ends - held, rest], axis=1).reshape(-1)
+
+
 def shards(
     features,
     neighbours,
@@ -395,6 +447,7 @@
     by_offset = neighbours[0].T
     local = by_offset + jnp.arange(4096, dtype=jnp.int32)[None, :]
     idx = by_tiles(jnp.where(by_offset < 0, -1, local))
+    plan = plan_of(counts[0])
     coarse_idx = by_tiles(coarse_neighbours[0].T)
 
     me = lax.axis_index("morton")
@@ -408,10 +461,10 @@
     codes = jnp.broadcast_to(edges[None], (8, 128))
     kept = jnp.where(destination == me, slot[0], 512)
 
-    (act,) = conv(False, idx, counts[0], lo, features[0], hi, w_first, gain_first[None])
+    (act,) = conv(False, idx, plan, counts[0], lo, features[0], hi, w_first, gain_first[None])
     lo, hi = halo_of(act)
     fine, rows, edge_rows = conv(
-        True, idx, counts[0], lo, act, hi, w_second, gain_second[None], features[0], w_down, gain_down[None], places=(kept,)
+        True, idx, plan, counts[0], lo, act, hi, w_second, gain_second[None], features[0], w_down, gain_down[None], places=(kept,)
     )
     pool, places = exchange(rows, edge_rows, codes)
     out = coarse(coarse_idx, places, pool, w_coarse, gain_coarse[None])

time: 234 us -> 177 us (0.76); the launches traced: 234 us -> 174 us
  Pallas kernels: 220 us -> 156 us
  other arithmetic: 3.55 us -> 6.45 us
    pallas_call x2, Pallas kernels: 174 us -> 112 us  [conv(): pl.pallas_call(functools.partial(conv_kernel, second), grid=(4,), in_spec...]
  transfers between devices with their start and end apart: 2 -> 2, of which waited for: 0 -> 0; matrix products, arithmetic and copies ran while one was open for 2% -> 4% of each run, Pallas kernels for 0% -> 0%
where the time goes in v3:
time: 177 us; the launch traced here: 174 us
  Pallas kernels  156 us (88%)
  other arithmetic  6.45 us (4%)
  starting transfers between devices  5.56 us (3%)
  local copies, waits for them, and re-layouts  5.09 us (3%)
    pallas_call x2, Pallas kernels, conv(): pl.pallas_call(functools.partial(conv_kernel, second), grid=(4,), in_spec...  112 us
    pallas_call x1, Pallas kernels, exchange(): pl.pallas_call(exchange_kernel, in_specs=[pl.BlockSpec(memory_space=pl.AN...  20.2 us
    pallas_call x1, Pallas kernels, coarse(): pl.pallas_call(coarse_kernel, in_specs=[pl.BlockSpec(memory_space=pltpu.S...  14.5 us
    pallas_call x1, Pallas kernels, halo_of(): pl.pallas_call(halo_kernel, in_specs=[pl.BlockSpec(memory_space=pl.ANY)],...  9.63 us
    ppermute x2, starting transfers between devices, shifted(): lax.ppermute(value, axis, [(source, source + steps) for source in range(i...  5.56 us
  transfers between devices with their start and end apart: 2, of which 0 were waited for; matrix products, arithmetic and copies ran while one was open for 4% of the time, Pallas kernels for 0%

profile of v3, /device:TPU:120, one launch (start us, length us, event | category | flops | bytes accessed | tf_op | source)
XLA Modules:
  0.0 174.0 jit_solution(1134292619398830768)
XLA Ops:
  0.6 0.7 slice_bitcast_fusion
  1.3 0.1 iota_compare_fusion.1
  1.4 0.1 lt.71
  1.5 0.1 lt.76
  1.6 1.4 bitcast_select_fusion
  3.0 1.9 %collective-permute-start = (bf16[1024,128]{1,0:T(8,128)(2,1)S(1)}, bf16[1024,128]{1,0:T(8,128)(2,1)S(1)}, u32[]{:S(2)}, u32[]{:S(2)}) collective-permute-start(bf16[1024,128]{1,0:T(8,128)(2,1)S(1)} %get-tuple-element.19), channel_id=1, source_target_pairs={{0,1},{1,2},{2,3},{3,4},{4,5},{5,6},{6,7},{7,8},{8,9},{9,10},{10,1... | collective-permute-start | bytes 786440 | tf_op jit(solution)/shard_map/ppermute | solution.py:24
  4.9 3.6 %collective-permute-start.1 = (bf16[1024,128]{1,0:T(8,128)(2,1)S(1)}, bf16[1024,128]{1,0:T(8,128)(2,1)S(1)}, u32[]{:S(2)}, u32[]{:S(2)}) collective-permute-start(bf16[1024,128]{1,0:T(8,128)(2,1)S(1)} %get-tuple-element.18), channel_id=1, source_target_pairs={{1,0},{2,1},{3,2},{4,3},{5,4},{6,5},{7,6},{8,7},{9,8},{10,9},{11,1... | collective-permute-start | bytes 786440 | tf_op jit(solution)/shard_map/ppermute | solution.py:24
  8.6 0.8 select_reduce_fusion.1
  9.4 1.3 convert_reduce_fusion
  10.8 0.7 sub.17
  11.4 0.2 slice_reduce_fusion
  11.7 0.1 broadcast_in_dim.109
  11.7 0.1 concatenate.6
  11.8 0.6 reshape.88.plan_ref
  12.5 1.3 fusion
  13.8 0.0 copy-start.2
  13.8 0.0 copy-start.3
  13.8 0.0 copy-start.4
  13.8 0.1 copy.30
  14.0 0.3 copy.40
  14.2 0.8 reshape.87.idx_ref
  15.1 0.0 copy-done.2
  15.1 0.6 reshape.90.idx_ref
  15.7 0.0 copy-done.3
  15.7 0.0 copy-done.4
  15.7 0.6 broadcast_add_fusion
  16.3 0.1 fusion.9
  16.4 0.1 pad_add_fusion
  16.5 0.0 collective-permute-done.lo_ref
  16.5 0.0 copy-start
  16.5 0.0 collective-permute-done.1.hi_ref
  16.5 0.0 copy-start.1
  16.5 0.7 copy-done
  17.2 0.1 copy-done.1
  17.3 54.4 %conv_first.1.field_ref.mid_ref = bf16[4096,128]{1,0:T(8,128)(2,1)} custom-call(s32[110592]{0:T(1024)} %reshape.87.idx_ref, s32[5120]{0:T(1024)} %reshape.88.plan_ref, s32[512]{0:T(512)} %bitcast.55, bf16[1024,128]{1,0:T(8,128)(2,1)} %copy-done, bf16[4096,128]{1,0:T(8,128)(2,1)} %bitcast.45, bf16[1024,128]{1,0:T(8,128)(2,1)} %copy-done.1, ...), custom_call_target="tpu_custom_call" | custom-call | tf_op jit(solution)/shard_map/conv_first/pallas_call | solution.py:215
  71.6 9.6 %halo.1 = (bf16[1024,128]{1,0:T(8,128)(2,1)}, bf16[1024,128]{1,0:T(8,128)(2,1)}) custom-call(bf16[4096,128]{1,0:T(8,128)(2,1)} %conv_first.1.field_ref.mid_ref), custom_call_target="tpu_custom_call" | custom-call | tf_op jit(solution)/shard_map/halo/pallas_call | solution.py:278
  81.3 57.4 %conv_second.1 = (bf16[4096,128]{1,0:T(8,128)(2,1)}, bf16[512,256]{1,0:T(8,128)(2,1)}, bf16[128,256]{1,0:T(8,128)(2,1)}) custom-call(s32[110592]{0:T(1024)} %reshape.87.idx_ref, s32[5120]{0:T(1024)} %reshape.88.plan_ref, s32[512]{0:T(512)} %bitcast.56, bf16[1024,128]{1,0:T(8,128)(2,1)} %get-tuple-element.9.lo_ref, ...), custom_call_target="tpu_custom_call" | custom-call | tf_op jit(solution)/shard_map/conv_second/pallas_call | solution.py:215
  138.7 0.6 broadcast_in_dim.119.codes_ref
  139.3 20.2 %exchange.1 = (bf16[4,640,256]{2,1,0:T(8,128)(2,1)}, s32[2,4,8,128]{3,2,1,0:T(8,128)}) custom-call(bf16[512,256]{1,0:T(8,128)(2,1)} %get-tuple-element.12.rows_ref, bf16[128,256]{1,0:T(8,128)(2,1)} %get-tuple-element.13.edge_ref, s32[8,128]{1,0:T(8,128)} %broadcast_in_dim.119.codes_ref), custom_call_target="tpu_custom_call" | custom-call | tf_op jit(solution)/shard_map/exchange/pallas_call | solution.py:328
  159.5 14.5 %coarse.1 = bf16[512,256]{1,0:T(8,128)(2,1)} custom-call(s32[13824]{0:T(1024)} %reshape.90.idx_ref, s32[2,4,8,128]{3,2,1,0:T(8,128)} %get-tuple-element.14.places_ref, bf16[4,640,256]{2,1,0:T(8,128)(2,1)} %get-tuple-element.15.pool_ref, bf16[6912,256]{1,0:T(8,128)(2,1)} %w_in.5, f32[1,256]{1,0:T(1,128)} %bitcast.59), custom_call_target="tpu_custom_call" | custom-call | tf_op jit(solution)/shard_map/coarse/pallas_call | solution.py:388
  (6 shorter events, 0.1 us)
Async XLA Ops:
  3.0 13.5 %collective-permute-start = (bf16[1024,128]{1,0:T(8,128)(2,1)S(1)}, bf16[1024,128]{1,0:T(8,128)(2,1)S(1)}, u32[]{:S(2)}, u32[]{:S(2)}) collective-permute-start(bf16[1024,128]{1,0:T(8,128)(2,1)S(1)} %get-tuple-element.19), channel_id=1, source_target_pairs={{0,1},{1,2},{2,3},{3,4},{4,5},{5,6},{6,7},{7,8},{8,9},{9,10},{10,1... | collective-permute-start | bytes 786440 | tf_op jit(solution)/shard_map/ppermute | solution.py:24
  4.9 11.6 %collective-permute-start.1 = (bf16[1024,128]{1,0:T(8,128)(2,1)S(1)}, bf16[1024,128]{1,0:T(8,128)(2,1)S(1)}, u32[]{:S(2)}, u32[]{:S(2)}) collective-permute-start(bf16[1024,128]{1,0:T(8,128)(2,1)S(1)} %get-tuple-element.18), channel_id=1, source_target_pairs={{1,0},{2,1},{3,2},{4,3},{5,4},{6,5},{7,6},{8,7},{9,8},{10,9},{11,1... | collective-permute-start | bytes 786440 | tf_op jit(solution)/shard_map/ppermute | solution.py:24
  13.8 1.3 copy-start.2
  13.8 1.9 %copy-start.3 = (s32[1,512]{1,0:T(1,128)S(1)}, s32[1,512]{1,0:T(1,128)}, u32[]{:S(2)}) copy-start(s32[1,512]{1,0:T(1,128)} %param.17) | copy-start | bytes 6148
  13.8 1.9 %copy-start.4 = (s32[1,512]{1,0:T(1,128)S(1)}, s32[1,512]{1,0:T(1,128)}, u32[]{:S(2)}) copy-start(s32[1,512]{1,0:T(1,128)} %param.18) | copy-start | bytes 6148
  16.5 0.7 copy-start
  16.5 0.8 copy-start.1

commit v4 on v3

--- a/solution.py
+++ b/solution.py
@@ -8,6 +8,8 @@
 from jax.sharding import PartitionSpec as P
 
 K = 27
+SELF = 13
+OTHERS = tuple(k for k in range(K) if k != SELF)
 TILE = 128
 GROUPS = TILE // 16
 PAD = 8
@@ -67,15 +69,15 @@
             listed = plan_ref.at[pl.ds(first + g * 16 + h * 8, 8)]
             at = [idx_ref.at[pl.ds(listed[i], (K - 1) * TILE + 1)] for i in range(8)]
             both.append([])
-            for k in range(K):
+            for n, k in enumerate(OTHERS):
                 acc = None
                 for i in range(8):
                     v = table[pl.ds(at[i][k * TILE] + (PAD - i), 8), :]
                     acc = v if i == 0 else jnp.where(masks[i], v, acc)
                 both[h].append(acc)
                 if h:
-                    dst_ref[pl.ds(pl.multiple_of(g * 16, 16), 16), k * 128 : k * 128 + 128] = jnp.concatenate(
-                        [both[0][k], acc], 0
+                    dst_ref[pl.ds(pl.multiple_of(g * 16, 16), 16), n * 128 : n * 128 + 128] = jnp.concatenate(
+                        [both[0][n], acc], 0
                     ).astype(jnp.bfloat16)
         return 0
 
@@ -99,9 +101,9 @@
     *rest,
 ):
     if second:
-        x_ref, wd_ref, gain_down_ref, place_ref, out_ref, down_ref, edge_ref, table, gathered, acc_ref, fine_ref, raw, placed = rest
+        x_ref, wd_ref, gain_down_ref, place_ref, out_ref, down_ref, edge_ref, table, gathered, acc_ref, w_ref, self_ref, fine_ref, raw, placed = rest
     else:
-        out_ref, table, gathered, acc_ref = rest
+        out_ref, table, gathered, acc_ref, w_ref, self_ref = rest
     step = pl.program_id(0)
     masks = sublane_masks()
     sub16 = lax.broadcasted_iota(jnp.int32, (8, 128), 0)
@@ -109,6 +111,8 @@
     @pl.when(step == 0)
     def _():
         table[:PAD, :] = jnp.zeros((PAD, 128), jnp.float32)
+        w_ref[: SELF * 128, :] = w_in[: SELF * 128, :]
+        w_ref[SELF * 128 :, :] = w_in[(SELF + 1) * 128 :, :]
         table[pl.ds(PAD, 1024), :] = lo_ref[...].astype(jnp.float32)
         if second:
             table[pl.ds(PAD + 1024, 4096), :] = mid_ref[...].astype(jnp.float32)
@@ -129,17 +133,20 @@
     plan = step * PLAN
     total = plan_ref[plan + LISTED + 128]
     gather_listed(idx_ref, plan_ref, plan, (total + 15) // 16, table, gathered, masks)
-    acc_ref[:MOSTLY, :] = jnp.dot(gathered[:MOSTLY, :], w_in[...], preferred_element_type=jnp.float32)
+    own = mid_ref[pl.ds(pl.multiple_of(step * 1024, 1024), 1024), :]
+    self_ref[...] = jnp.dot(own, w_in[SELF * 128 : (SELF + 1) * 128, :], preferred_element_type=jnp.float32)
+    acc_ref[:MOSTLY, :] = jnp.dot(gathered[:MOSTLY, :], w_ref[...], preferred_element_type=jnp.float32)
 
     @pl.when(total > MOSTLY)
     def _():
-        acc_ref[MOSTLY:1024, :] = jnp.dot(gathered[MOSTLY:, :], w_in[...], preferred_element_type=jnp.float32)
+        acc_ref[MOSTLY:1024, :] = jnp.dot(gathered[MOSTLY:, :], w_ref[...], preferred_element_type=jnp.float32)
 
     def epilogue(tile, _):
         gain = gain_ref[...]
         for i in range(GROUPS):
             start = plan_ref.at[pl.ds(plan + LISTED + tile * GROUPS * 2 + 2 * i, 2)]
-            h = normed(jnp.concatenate([acc_ref[pl.ds(start[0], 8), :], acc_ref[pl.ds(start[1], 8), :]], 0), gain)
+            h = jnp.concatenate([acc_ref[pl.ds(start[0], 8), :], acc_ref[pl.ds(start[1], 8), :]], 0)
+            h = normed(h + self_ref[pl.ds(pl.multiple_of(tile * TILE + i * 16, 16), 16), :], gain)
             row = pl.multiple_of(step * 1024 + tile * TILE + i * 16, 16)
             if second:
                 h = x_ref[pl.ds(row, 16), :].astype(jnp.float32) + h
@@ -203,8 +210,10 @@
     out_shape = [jax.ShapeDtypeStruct((4096, 128), jnp.bfloat16)]
     scratch = [
         pltpu.VMEM((PAD + 6144 + 8, 128), jnp.float32),
-        pltpu.VMEM((1024, K * 128), jnp.bfloat16),
+        pltpu.VMEM((1024, len(OTHERS) * 128), jnp.bfloat16),
         pltpu.VMEM((1024 + 8, 128), jnp.float32),
+        pltpu.VMEM((len(OTHERS) * 128, 128), jnp.bfloat16),
+        pltpu.VMEM((1024, 128), jnp.float32),
     ]
     if second:
         out_shape.append(jax.ShapeDtypeStruct((512, 256), jnp.bfloat16))
@@ -402,8 +411,7 @@
 
 
 def by_tiles(index):
-    rows = index.shape[1]
-    return index.reshape(K, rows // TILE, TILE).transpose(1, 0, 2).reshape(-1)
+    return index.reshape(K, -1, 1, TILE).transpose(1, 0, 2, 3).reshape(-1)
 
 
 def plan_of(counts):

time: 177 us -> 176 us (level)
    pallas_call x1, Pallas kernels: 9.63 us -> 6.8 us  [halo_of(): pl.pallas_call(halo_kernel, in_specs=[pl.BlockSpec(memory_space=pl.ANY)],...]
  transfers between devices with their start and end apart: 2 -> 2, of which waited for: 0 -> 0; matrix products, arithmetic and copies ran while one was open for 4% -> 5% of each run, Pallas kernels for 0% -> 0%
where the time goes in v4:
time: 176 us; the launch traced here: 173 us
  Pallas kernels  156 us (89%)
  other arithmetic  6.45 us (4%)
  starting transfers between devices  5.56 us (3%)
  local copies, waits for them, and re-layouts  5.09 us (3%)
    pallas_call x2, Pallas kernels, conv(): pl.pallas_call(functools.partial(conv_kernel, second), grid=(4,), in_spec...  113 us
    pallas_call x1, Pallas kernels, exchange(): pl.pallas_call(exchange_kernel, in_specs=[pl.BlockSpec(memory_space=pl.AN...  21.5 us
    pallas_call x1, Pallas kernels, coarse(): pl.pallas_call(coarse_kernel, in_specs=[pl.BlockSpec(memory_space=pltpu.S...  14.5 us
    pallas_call x1, Pallas kernels, halo_of(): pl.pallas_call(halo_kernel, in_specs=[pl.BlockSpec(memory_space=pl.ANY)],...  6.8 us
    ppermute x2, starting transfers between devices, shifted(): lax.ppermute(value, axis, [(source, source + steps) for source in range(i...  5.56 us
  transfers between devices with their start and end apart: 2, of which 0 were waited for; matrix products, arithmetic and copies ran while one was open for 5% of the time, Pallas kernels for 0%

profile of v4, /device:TPU:120, one launch (start us, length us, event | category | flops | bytes accessed | tf_op | source)
XLA Modules:
  0.0 173.4 jit_solution(12283945480717945153)
XLA Ops:
  0.6 0.7 slice_bitcast_fusion.1
  1.3 0.1 iota_compare_fusion.1
  1.4 0.1 lt.71
  1.5 0.1 lt.76
  1.6 1.4 bitcast_select_fusion
  3.0 1.9 %collective-permute-start = (bf16[1024,128]{1,0:T(8,128)(2,1)S(1)}, bf16[1024,128]{1,0:T(8,128)(2,1)S(1)}, u32[]{:S(2)}, u32[]{:S(2)}) collective-permute-start(bf16[1024,128]{1,0:T(8,128)(2,1)S(1)} %get-tuple-element.19), channel_id=1, source_target_pairs={{0,1},{1,2},{2,3},{3,4},{4,5},{5,6},{6,7},{7,8},{8,9},{9,10},{10,1... | collective-permute-start | bytes 786440 | tf_op jit(solution)/shard_map/ppermute | solution.py:26
  4.9 3.6 %collective-permute-start.1 = (bf16[1024,128]{1,0:T(8,128)(2,1)S(1)}, bf16[1024,128]{1,0:T(8,128)(2,1)S(1)}, u32[]{:S(2)}, u32[]{:S(2)}) collective-permute-start(bf16[1024,128]{1,0:T(8,128)(2,1)S(1)} %get-tuple-element.18), channel_id=1, source_target_pairs={{1,0},{2,1},{3,2},{4,3},{5,4},{6,5},{7,6},{8,7},{9,8},{10,9},{11,1... | collective-permute-start | bytes 786440 | tf_op jit(solution)/shard_map/ppermute | solution.py:26
  8.6 0.8 select_reduce_fusion.1
  9.4 1.3 convert_reduce_fusion
  10.8 0.7 sub.17
  11.4 0.2 slice_reduce_fusion
  11.7 0.1 broadcast_in_dim.109
  11.7 0.1 concatenate.6
  11.8 0.6 reshape.88.plan_ref
  12.5 1.3 fusion
  13.8 0.0 copy-start.2
  13.8 0.0 copy-start.3
  13.8 0.0 copy-start.4
  13.8 0.1 copy.30
  14.0 0.3 copy.40
  14.2 0.8 reshape.87.idx_ref
  15.1 0.0 copy-done.2
  15.1 0.6 reshape.90.idx_ref
  15.7 0.0 copy-done.3
  15.7 0.0 copy-done.4
  15.7 0.6 broadcast_add_fusion
  16.3 0.1 fusion.9
  16.4 0.1 pad_add_fusion
  16.5 0.0 collective-permute-done.lo_ref
  16.5 0.0 copy-start
  16.5 0.0 collective-permute-done.1.hi_ref
  16.5 0.0 copy-start.1
  16.5 0.7 copy-done
  17.2 0.1 copy-done.1
  17.3 54.9 %conv_first.1.field_ref.mid_ref = bf16[4096,128]{1,0:T(8,128)(2,1)} custom-call(s32[110592]{0:T(1024)} %reshape.87.idx_ref, s32[5120]{0:T(1024)} %reshape.88.plan_ref, s32[512]{0:T(512)} %bitcast.62, bf16[1024,128]{1,0:T(8,128)(2,1)} %copy-done, bf16[4096,128]{1,0:T(8,128)(2,1)} %bitcast.52, bf16[1024,128]{1,0:T(8,128)(2,1)} %copy-done.1, ...), custom_call_target="tpu_custom_call" | custom-call | tf_op jit(solution)/shard_map/conv_first/pallas_call | solution.py:224
  72.2 6.8 %halo.1 = (bf16[1024,128]{1,0:T(8,128)(2,1)}, bf16[1024,128]{1,0:T(8,128)(2,1)}) custom-call(bf16[4096,128]{1,0:T(8,128)(2,1)} %conv_first.1.field_ref.mid_ref), custom_call_target="tpu_custom_call" | custom-call | tf_op jit(solution)/shard_map/halo/pallas_call | solution.py:287
  79.0 57.9 %conv_second.1 = (bf16[4096,128]{1,0:T(8,128)(2,1)}, bf16[512,256]{1,0:T(8,128)(2,1)}, bf16[128,256]{1,0:T(8,128)(2,1)}) custom-call(s32[110592]{0:T(1024)} %reshape.87.idx_ref, s32[5120]{0:T(1024)} %reshape.88.plan_ref, s32[512]{0:T(512)} %bitcast.63, bf16[1024,128]{1,0:T(8,128)(2,1)} %get-tuple-element.9.lo_ref, ...), custom_call_target="tpu_custom_call" | custom-call | tf_op jit(solution)/shard_map/conv_second/pallas_call | solution.py:224
  136.8 0.6 broadcast_in_dim.119.codes_ref
  137.4 21.5 %exchange.1 = (bf16[4,640,256]{2,1,0:T(8,128)(2,1)}, s32[2,4,8,128]{3,2,1,0:T(8,128)}) custom-call(bf16[512,256]{1,0:T(8,128)(2,1)} %get-tuple-element.12.rows_ref, bf16[128,256]{1,0:T(8,128)(2,1)} %get-tuple-element.13.edge_ref, s32[8,128]{1,0:T(8,128)} %broadcast_in_dim.119.codes_ref), custom_call_target="tpu_custom_call" | custom-call | tf_op jit(solution)/shard_map/exchange/pallas_call | solution.py:337
  158.9 14.5 %coarse.1 = bf16[512,256]{1,0:T(8,128)(2,1)} custom-call(s32[13824]{0:T(1024)} %reshape.90.idx_ref, s32[2,4,8,128]{3,2,1,0:T(8,128)} %get-tuple-element.14.places_ref, bf16[4,640,256]{2,1,0:T(8,128)(2,1)} %get-tuple-element.15.pool_ref, bf16[6912,256]{1,0:T(8,128)(2,1)} %w_in.5, f32[1,256]{1,0:T(1,128)} %bitcast.66), custom_call_target="tpu_custom_call" | custom-call | tf_op jit(solution)/shard_map/coarse/pallas_call | solution.py:397
  (6 shorter events, 0.1 us)
Async XLA Ops:
  3.0 13.5 %collective-permute-start = (bf16[1024,128]{1,0:T(8,128)(2,1)S(1)}, bf16[1024,128]{1,0:T(8,128)(2,1)S(1)}, u32[]{:S(2)}, u32[]{:S(2)}) collective-permute-start(bf16[1024,128]{1,0:T(8,128)(2,1)S(1)} %get-tuple-element.19), channel_id=1, source_target_pairs={{0,1},{1,2},{2,3},{3,4},{4,5},{5,6},{6,7},{7,8},{8,9},{9,10},{10,1... | collective-permute-start | bytes 786440 | tf_op jit(solution)/shard_map/ppermute | solution.py:26
  4.9 11.6 %collective-permute-start.1 = (bf16[1024,128]{1,0:T(8,128)(2,1)S(1)}, bf16[1024,128]{1,0:T(8,128)(2,1)S(1)}, u32[]{:S(2)}, u32[]{:S(2)}) collective-permute-start(bf16[1024,128]{1,0:T(8,128)(2,1)S(1)} %get-tuple-element.18), channel_id=1, source_target_pairs={{1,0},{2,1},{3,2},{4,3},{5,4},{6,5},{7,6},{8,7},{9,8},{10,9},{11,1... | collective-permute-start | bytes 786440 | tf_op jit(solution)/shard_map/ppermute | solution.py:26
  13.8 1.3 copy-start.2
  13.8 1.9 %copy-start.3 = (s32[1,512]{1,0:T(1,128)S(1)}, s32[1,512]{1,0:T(1,128)}, u32[]{:S(2)}) copy-start(s32[1,512]{1,0:T(1,128)} %param.17) | copy-start | bytes 6148
  13.8 1.9 %copy-start.4 = (s32[1,512]{1,0:T(1,128)S(1)}, s32[1,512]{1,0:T(1,128)}, u32[]{:S(2)}) copy-start(s32[1,512]{1,0:T(1,128)} %param.18) | copy-start | bytes 6148
  16.5 0.7 copy-start
  16.5 0.8 copy-start.1

commit v5 on v4

--- a/solution.py
+++ b/solution.py
@@ -17,7 +17,7 @@
 LISTED = 1056
 MOSTLY = 640
 EPS = 1e-05
-VMEM_LIMIT = 58 * 2**20
+VMEM_LIMIT = 34 * 2**20
 
 
 def shifted(value, axis, steps):

time: 176 us -> 187 us (1.062); the launches traced: 173 us -> 186 us
  local copies, waits for them, and re-layouts: 5.09 us -> 16.7 us
    unnamed x12 -> x52, local copies, waits for them, and re-layouts: 0.9 us -> 13.9 us
    pallas_call x1, Pallas kernels: 6.8 us -> 9.77 us  [halo_of(): pl.pallas_call(halo_kernel, in_specs=[pl.BlockSpec(memory_space=pl.ANY)],...]
    pallas_call x2, Pallas kernels: 113 us -> 110 us  [conv(): pl.pallas_call(functools.partial(conv_kernel, second), grid=(4,), in_spec...]
  transfers between devices with their start and end apart: 2 -> 2, of which waited for: 0 -> 0; matrix products, arithmetic and copies ran while one was open for 5% -> 3% of each run, Pallas kernels for 0% -> 0%
where the time goes in v5:
time: 187 us; the launch traced here: 186 us
  Pallas kernels  156 us (83%)
  local copies, waits for them, and re-layouts  16.7 us (9%)
  other arithmetic  7.23 us (4%)
  starting transfers between devices  5.55 us (3%)
    pallas_call x2, Pallas kernels, conv(): pl.pallas_call(functools.partial(conv_kernel, second), grid=(4,), in_spec...  110 us
    pallas_call x1, Pallas kernels, exchange(): pl.pallas_call(exchange_kernel, in_specs=[pl.BlockSpec(memory_space=pl.AN...  22.1 us
    pallas_call x1, Pallas kernels, coarse(): pl.pallas_call(coarse_kernel, in_specs=[pl.BlockSpec(memory_space=pltpu.S...  14.1 us
    unnamed x52, local copies, waits for them, and re-layouts  13.9 us
    pallas_call x1, Pallas kernels, halo_of(): pl.pallas_call(halo_kernel, in_specs=[pl.BlockSpec(memory_space=pl.ANY)],...  9.77 us
    ppermute x2, starting transfers between devices, shifted(): lax.ppermute(value, axis, [(source, source + steps) for source in range(i...  5.55 us
  transfers between devices with their start and end apart: 2, of which 0 were waited for; matrix products, arithmetic and copies ran while one was open for 3% of the time, Pallas kernels for 0%

profile of v5, /device:TPU:120, one launch (start us, length us, event | category | flops | bytes accessed | tf_op | source)
XLA Modules:
  0.0 186.3 jit_solution(10161594918485999233)
XLA Ops:
  0.6 0.7 slice_bitcast_fusion.1
  1.3 0.1 iota_compare_fusion.1
  1.4 0.1 lt.71
  1.5 0.1 lt.76
  1.6 2.2 %bitcast_select_fusion = (bf16[1024,128]{1,0:T(8,128)(2,1)}, bf16[1024,128]{1,0:T(8,128)(2,1)}) fusion(bf16[1,4096,128]{2,1,0:T(8,128)(2,1)} %param.14, pred[1024]{0:T(1024)(128)(4,1)S(1)} %lt.76, pred[1024]{0:T(1024)(128)(4,1)S(1)} %lt.71), kind=kLoop, calls=%fused_computation.8 | loop fusion | flops 262144 | bytes 1050624 | tf_op jit(solution)/shard_map/jit(_where)/select_n | solution.py:452
  3.8 1.9 %collective-permute-start = (bf16[1024,128]{1,0:T(8,128)(2,1)}, bf16[1024,128]{1,0:T(8,128)(2,1)S(1)}, u32[]{:S(2)}, u32[]{:S(2)}) collective-permute-start(bf16[1024,128]{1,0:T(8,128)(2,1)} %get-tuple-element.19), channel_id=1, source_target_pairs={{0,1},{1,2},{2,3},{3,4},{4,5},{5,6},{6,7},{7,8},{8,9},{9,10},{10,1... | collective-permute-start | bytes 786440 | tf_op jit(solution)/shard_map/ppermute | solution.py:26
  5.7 3.6 %collective-permute-start.1 = (bf16[1024,128]{1,0:T(8,128)(2,1)}, bf16[1024,128]{1,0:T(8,128)(2,1)S(1)}, u32[]{:S(2)}, u32[]{:S(2)}) collective-permute-start(bf16[1024,128]{1,0:T(8,128)(2,1)} %get-tuple-element.18), channel_id=1, source_target_pairs={{1,0},{2,1},{3,2},{4,3},{5,4},{6,5},{7,6},{8,7},{9,8},{10,9},{11,1... | collective-permute-start | bytes 786440 | tf_op jit(solution)/shard_map/ppermute | solution.py:26
  9.4 0.8 select_reduce_fusion.1
  10.2 1.3 convert_reduce_fusion
  11.5 0.7 sub.17
  12.2 0.2 slice_reduce_fusion
  12.5 0.1 broadcast_in_dim.109
  12.5 0.1 concatenate.6
  12.6 1.3 fusion
  14.0 0.0 copy-start.21
  14.0 0.0 copy-start.22
  14.0 0.0 copy-start.23
  14.0 0.0 copy-start.2
  14.0 0.0 copy-start.5
  14.0 0.0 copy-start.15
  14.0 0.1 copy.30
  14.2 0.3 copy.40
  14.5 0.3 copy-done.21
  14.8 0.6 reshape.90.idx_ref
  15.5 0.0 copy-done.22
  15.5 0.0 copy-done.23
  15.5 0.1 fusion.9
  15.6 0.7 pad_add_fusion
  16.2 0.0 collective-permute-done.lo_ref
  16.2 0.0 collective-permute-done.1.hi_ref
  16.2 0.0 copy-start.8
  16.2 0.7 copy-done.8
  16.9 0.0 copy-done.2
  16.9 0.0 copy-done.5
  16.9 0.0 copy-done.15
  16.9 0.0 copy-start.9
  16.9 0.9 copy-done.9
  17.9 0.0 copy-start.19
  17.9 0.7 copy-done.19
  18.5 53.1 %conv_first.1.field_ref.mid_ref = bf16[4096,128]{1,0:T(8,128)(2,1)S(1)} custom-call(s32[110592]{0:T(1024)S(1)} %reshape.87.idx_ref, s32[5120]{0:T(1024)S(1)} %reshape.88.plan_ref, s32[512]{0:T(512)S(1)} %bitcast.56, bf16[1024,128]{1,0:T(8,128)(2,1)S(1)} %collective-permute-done.lo_ref, bf16[4096,128]{1,0:T(8,128)(2,1)S(1)} %bitcast.52, ...), custom_call_target="tpu_custom_call" | custom-call | tf_op jit(solution)/shard_map/conv_first/pallas_call | solution.py:224
  71.6 0.0 copy-start
  71.6 1.0 copy-done
  72.6 9.8 %halo.1 = (bf16[1024,128]{1,0:T(8,128)(2,1)}, bf16[1024,128]{1,0:T(8,128)(2,1)}) custom-call(bf16[4096,128]{1,0:T(8,128)(2,1)} %copy-done), custom_call_target="tpu_custom_call" | custom-call | tf_op jit(solution)/shard_map/halo/pallas_call | solution.py:287
  82.4 0.0 copy-done.6
  82.4 0.0 copy-done.17
  82.4 0.0 copy-start.1
  82.4 1.2 copy-done.1
  83.6 1.0 copy-done.7
  84.7 0.9 copy-done.11
  85.6 0.9 copy-done.12
  86.6 0.7 copy-done.20
  87.2 56.9 %conv_second.1 = (bf16[4096,128]{1,0:T(8,128)(2,1)}, bf16[512,256]{1,0:T(8,128)(2,1)S(1)}, bf16[128,256]{1,0:T(8,128)(2,1)S(1)}) custom-call(s32[110592]{0:T(1024)S(1)} %reshape.87.idx_ref, s32[5120]{0:T(1024)S(1)} %reshape.88.plan_ref, s32[512]{0:T(512)S(1)} %bitcast.57, bf16[1024,128]{1,0:T(8,128)(2,1)S(1)} %copy-done.11, bf16[4096,128]{1,0:T(8,128)(2,1)S(1)} %copy-done.1, ...), custom_call_target="tpu_custom_call" | custom-call | tf_op jit(solution)/shard_map/conv_second/pallas_call | solution.py:224
  144.1 0.7 copy-done.10
  144.8 0.6 copy-done.14
  145.4 0.0 copy-done.24
  145.4 0.6 broadcast_in_dim.119.codes_ref
  146.0 22.1 %exchange.1 = (bf16[4,640,256]{2,1,0:T(8,128)(2,1)}, s32[2,4,8,128]{3,2,1,0:T(8,128)}) custom-call(bf16[512,256]{1,0:T(8,128)(2,1)} %copy-done.10, bf16[128,256]{1,0:T(8,128)(2,1)} %copy-done.14, s32[8,128]{1,0:T(8,128)} %broadcast_in_dim.119.codes_ref), custom_call_target="tpu_custom_call" | custom-call | tf_op jit(solution)/shard_map/exchange/pallas_call | solution.py:337
  168.2 0.0 copy-done.13
  168.2 0.0 copy-done.18
  168.2 0.0 copy-start.3
  168.2 2.0 %copy-done.3 = bf16[6912,256]{1,0:T(8,128)(2,1)S(1)} copy-done((bf16[6912,256]{1,0:T(8,128)(2,1)S(1)}, bf16[6912,256]{1,0:T(8,128)(2,1)}, u32[]{:S(2)}) %copy-start.3) | copy-done | bytes 3538968
  170.2 1.3 copy-done.4
  171.5 0.8 copy-done.16
  172.3 14.1 %coarse.1 = bf16[512,256]{1,0:T(8,128)(2,1)} custom-call(s32[13824]{0:T(1024)S(1)} %copy-done.13, s32[2,4,8,128]{3,2,1,0:T(8,128)S(1)} %copy-done.16, bf16[4,640,256]{2,1,0:T(8,128)(2,1)S(1)} %copy-done.4, bf16[6912,256]{1,0:T(8,128)(2,1)S(1)} %copy-done.3, f32[1,256]{1,0:T(1,128)S(1)} %bitcast.60), custom_call_target="tpu_custom_call" | custom-call | tf_op jit(solution)/shard_map/coarse/pallas_call | solution.py:397
  (22 shorter events, 0.2 us)
Async XLA Ops:
  3.8 12.4 %collective-permute-start = (bf16[1024,128]{1,0:T(8,128)(2,1)}, bf16[1024,128]{1,0:T(8,128)(2,1)S(1)}, u32[]{:S(2)}, u32[]{:S(2)}) collective-permute-start(bf16[1024,128]{1,0:T(8,128)(2,1)} %get-tuple-element.19), channel_id=1, source_target_pairs={{0,1},{1,2},{2,3},{3,4},{4,5},{5,6},{6,7},{7,8},{8,9},{9,10},{10,1... | collective-permute-start | bytes 786440 | tf_op jit(solution)/shard_map/ppermute | solution.py:26
  5.7 10.5 %collective-permute-start.1 = (bf16[1024,128]{1,0:T(8,128)(2,1)}, bf16[1024,128]{1,0:T(8,128)(2,1)S(1)}, u32[]{:S(2)}, u32[]{:S(2)}) collective-permute-start(bf16[1024,128]{1,0:T(8,128)(2,1)} %get-tuple-element.18), channel_id=1, source_target_pairs={{1,0},{2,1},{3,2},{4,3},{5,4},{6,5},{7,6},{8,7},{9,8},{10,9},{11,1... | collective-permute-start | bytes 786440 | tf_op jit(solution)/shard_map/ppermute | solution.py:26
  14.0 0.8 copy-start.21
  14.0 1.5 copy-start.22
  14.0 1.5 copy-start.23
  14.0 2.9 %copy-start.2 = (bf16[1,4096,128]{2,1,0:T(8,128)(2,1)S(1)}, bf16[1,4096,128]{2,1,0:T(8,128)(2,1)}, u32[]{:S(2)}) copy-start(bf16[1,4096,128]{2,1,0:T(8,128)(2,1)} %param.14) | copy-start | bytes 3145732
  14.0 2.9 %copy-start.5 = (bf16[3456,128]{1,0:T(8,128)(2,1)S(1)}, bf16[3456,128]{1,0:T(8,128)(2,1)}, u32[]{:S(2)}) copy-start(bf16[3456,128]{1,0:T(8,128)(2,1)} %w_in.3) | copy-start | bytes 2654212
  14.0 2.9 %copy-start.15 = (s32[1,512]{1,0:T(1,128)S(1)}, s32[1,512]{1,0:T(1,128)}, u32[]{:S(2)}) copy-start(s32[1,512]{1,0:T(1,128)} %param.16) | copy-start | bytes 6148
  16.2 0.7 copy-start.8
  16.9 1.0 copy-start.9
  17.9 0.7 copy-start.19
  18.5 63.8 %copy-start.6 = (bf16[3456,128]{1,0:T(8,128)(2,1)S(1)}, bf16[3456,128]{1,0:T(8,128)(2,1)}, u32[]{:S(2)}) copy-start(bf16[3456,128]{1,0:T(8,128)(2,1)} %w_in.4) | copy-start | bytes 2654212
  18.5 63.9 %copy-start.17 = (f32[256]{0:T(256)S(1)}, f32[256]{0:T(256)}, u32[]{:S(2)}) copy-start(f32[256]{0:T(256)} %param.26) | copy-start | bytes 3076
  71.6 1.0 copy-start
  82.4 1.2 copy-start.1
  83.6 1.0 copy-start.7
  84.7 0.9 copy-start.11
  85.6 0.9 copy-start.12
  86.6 0.7 copy-start.20
  87.2 58.2 %copy-start.24 = (s32[128]{0:T(128)S(1)}, s32[128]{0:T(128)}, u32[]{:S(2)}) copy-start(s32[128]{0:T(128)} %pad_add_fusion) | copy-start | bytes 1540
  87.2 80.9 %copy-start.13 = (s32[13824]{0:T(1024)S(1)}, s32[13824]{0:T(1024)}, u32[]{:S(2)}) copy-start(s32[13824]{0:T(1024)} %reshape.90.idx_ref) | copy-start | bytes 165892
  87.2 80.9 %copy-start.18 = (f32[256]{0:T(256)S(1)}, f32[256]{0:T(256)}, u32[]{:S(2)}) copy-start(f32[256]{0:T(256)} %param.27) | copy-start | bytes 3076
  144.1 0.7 copy-start.10
  144.8 0.6 copy-start.14
  168.2 2.0 %copy-start.3 = (bf16[6912,256]{1,0:T(8,128)(2,1)S(1)}, bf16[6912,256]{1,0:T(8,128)(2,1)}, u32[]{:S(2)}) copy-start(bf16[6912,256]{1,0:T(8,128)(2,1)} %w_in.5) | copy-start | bytes 10616836
  170.2 1.3 copy-start.4
  171.5 0.8 copy-start.16

commit v6 on v4

--- a/solution.py
+++ b/solution.py
@@ -340,7 +340,7 @@
         out_specs=[pl.BlockSpec(memory_space=pl.ANY)] * 2,
         out_shape=[
             jax.ShapeDtypeStruct((4, REACH, 256), jnp.bfloat16),
-            jax.ShapeDtypeStruct((2, 4, 8, 128), jnp.int32),
+            jax.ShapeDtypeStruct((2, 4, 1, 128), jnp.int32),
         ],
         scratch_shapes=[
             pltpu.SemaphoreType.DMA((22,)),
@@ -466,7 +466,7 @@
         return jnp.where(destination == to, at, NOWHERE)
 
     edges = jnp.concatenate([handed(me + 1)[448:], handed(me - 1)[:64]])
-    codes = jnp.broadcast_to(edges[None], (8, 128))
+    codes = edges[None]
     kept = jnp.where(destination == me, slot[0], 512)
 
     (act,) = conv(False, idx, plan, counts[0], lo, features[0], hi, w_first, gain_first[None])

time: 176 us -> 174 us (0.989); the launches traced: 173 us -> 174 us
  no operation moved by 1% of the time
where the time goes in v6:
time: 174 us
  Pallas kernels  156 us (90%)
  other arithmetic  7.03 us (4%)
  starting transfers between devices  5.56 us (3%)
  local copies, waits for them, and re-layouts  4.5 us (3%)
    pallas_call x2, Pallas kernels, conv(): pl.pallas_call(functools.partial(conv_kernel, second), grid=(4,), in_spec...  114 us
    pallas_call x1, Pallas kernels, exchange(): pl.pallas_call(exchange_kernel, in_specs=[pl.BlockSpec(memory_space=pl.AN...  20.7 us
    pallas_call x1, Pallas kernels, coarse(): pl.pallas_call(coarse_kernel, in_specs=[pl.BlockSpec(memory_space=pltpu.S...  14.5 us
    pallas_call x1, Pallas kernels, halo_of(): pl.pallas_call(halo_kernel, in_specs=[pl.BlockSpec(memory_space=pl.ANY)],...  6.15 us
    ppermute x2, starting transfers between devices, shifted(): lax.ppermute(value, axis, [(source, source + steps) for source in range(i...  5.56 us
  transfers between devices with their start and end apart: 2, of which 0 were waited for; matrix products, arithmetic and copies ran while one was open for 5% of the time, Pallas kernels for 0%

profile of v6, /device:TPU:120, one launch (start us, length us, event | category | flops | bytes accessed | tf_op | source)
XLA Modules:
  0.0 173.6 jit_solution(10449111572678105783)
XLA Ops:
  0.6 0.7 slice_bitcast_fusion.1
  1.3 0.1 iota_compare_fusion.1
  1.4 0.1 lt.71
  1.5 0.1 lt.76
  1.6 1.4 bitcast_select_fusion
  3.0 1.9 %collective-permute-start = (bf16[1024,128]{1,0:T(8,128)(2,1)S(1)}, bf16[1024,128]{1,0:T(8,128)(2,1)S(1)}, u32[]{:S(2)}, u32[]{:S(2)}) collective-permute-start(bf16[1024,128]{1,0:T(8,128)(2,1)S(1)} %get-tuple-element.19), channel_id=1, source_target_pairs={{0,1},{1,2},{2,3},{3,4},{4,5},{5,6},{6,7},{7,8},{8,9},{9,10},{10,1... | collective-permute-start | bytes 786440 | tf_op jit(solution)/shard_map/ppermute | solution.py:26
  4.9 3.6 %collective-permute-start.1 = (bf16[1024,128]{1,0:T(8,128)(2,1)S(1)}, bf16[1024,128]{1,0:T(8,128)(2,1)S(1)}, u32[]{:S(2)}, u32[]{:S(2)}) collective-permute-start(bf16[1024,128]{1,0:T(8,128)(2,1)S(1)} %get-tuple-element.18), channel_id=1, source_target_pairs={{1,0},{2,1},{3,2},{4,3},{5,4},{6,5},{7,6},{8,7},{9,8},{10,9},{11,1... | collective-permute-start | bytes 786440 | tf_op jit(solution)/shard_map/ppermute | solution.py:26
  8.6 0.8 select_reduce_fusion.1
  9.4 1.3 convert_reduce_fusion
  10.8 0.7 sub.17
  11.4 0.2 slice_reduce_fusion
  11.7 0.1 broadcast_in_dim.106
  11.7 0.1 concatenate.6
  11.8 0.6 reshape.87.plan_ref
  12.5 1.3 fusion
  13.8 0.0 copy-start.2
  13.8 0.0 copy-start.3
  13.8 0.0 copy-start.4
  13.8 0.1 copy.30
  14.0 0.3 copy.40
  14.2 0.8 reshape.86.idx_ref
  15.1 0.0 copy-done.2
  15.1 0.6 reshape.89.idx_ref
  15.7 0.0 copy-done.3
  15.7 0.0 copy-done.4
  15.7 0.6 broadcast_add_fusion
  16.3 0.1 fusion.9
  16.4 0.7 add_bitcast_fusion.codes_ref
  17.1 0.0 collective-permute-done.lo_ref
  17.1 0.0 copy-start
  17.1 0.0 collective-permute-done.1.hi_ref
  17.1 0.0 copy-start.1
  17.1 0.7 copy-done
  17.8 0.1 copy-done.1
  17.9 55.7 %conv_first.1.field_ref.mid_ref = bf16[4096,128]{1,0:T(8,128)(2,1)} custom-call(s32[110592]{0:T(1024)} %reshape.86.idx_ref, s32[5120]{0:T(1024)} %reshape.87.plan_ref, s32[512]{0:T(512)} %bitcast.64, bf16[1024,128]{1,0:T(8,128)(2,1)} %copy-done, bf16[4096,128]{1,0:T(8,128)(2,1)} %bitcast.54, bf16[1024,128]{1,0:T(8,128)(2,1)} %copy-done.1, ...), custom_call_target="tpu_custom_call" | custom-call | tf_op jit(solution)/shard_map/conv_first/pallas_call | solution.py:224
  73.6 6.2 %halo.1 = (bf16[1024,128]{1,0:T(8,128)(2,1)}, bf16[1024,128]{1,0:T(8,128)(2,1)}) custom-call(bf16[4096,128]{1,0:T(8,128)(2,1)} %conv_first.1.field_ref.mid_ref), custom_call_target="tpu_custom_call" | custom-call | tf_op jit(solution)/shard_map/halo/pallas_call | solution.py:287
  79.7 58.7 %conv_second.1 = (bf16[4096,128]{1,0:T(8,128)(2,1)}, bf16[512,256]{1,0:T(8,128)(2,1)}, bf16[128,256]{1,0:T(8,128)(2,1)}) custom-call(s32[110592]{0:T(1024)} %reshape.86.idx_ref, s32[5120]{0:T(1024)} %reshape.87.plan_ref, s32[512]{0:T(512)} %bitcast.65, bf16[1024,128]{1,0:T(8,128)(2,1)} %get-tuple-element.9.lo_ref, ...), custom_call_target="tpu_custom_call" | custom-call | tf_op jit(solution)/shard_map/conv_second/pallas_call | solution.py:224
  138.4 20.7 %exchange.1 = (bf16[4,640,256]{2,1,0:T(8,128)(2,1)}, s32[2,4,1,128]{3,2,1,0:T(1,128)}) custom-call(bf16[512,256]{1,0:T(8,128)(2,1)} %get-tuple-element.12.rows_ref, bf16[128,256]{1,0:T(8,128)(2,1)} %get-tuple-element.13.edge_ref, s32[1,128]{1,0:T(1,128)} %add_bitcast_fusion.codes_ref), custom_call_target="tpu_custom_call" | custom-call | tf_op jit(solution)/shard_map/exchange/pallas_call | solution.py:337
  159.1 14.5 %coarse.1 = bf16[512,256]{1,0:T(8,128)(2,1)} custom-call(s32[13824]{0:T(1024)} %reshape.89.idx_ref, s32[2,4,1,128]{3,2,1,0:T(1,128)} %get-tuple-element.14.places_ref, bf16[4,640,256]{2,1,0:T(8,128)(2,1)} %get-tuple-element.15.pool_ref, bf16[6912,256]{1,0:T(8,128)(2,1)} %w_in.5, f32[1,256]{1,0:T(1,128)} %bitcast.67), custom_call_target="tpu_custom_call" | custom-call | tf_op jit(solution)/shard_map/coarse/pallas_call | solution.py:397
  (6 shorter events, 0.1 us)
Async XLA Ops:
  3.0 14.1 %collective-permute-start = (bf16[1024,128]{1,0:T(8,128)(2,1)S(1)}, bf16[1024,128]{1,0:T(8,128)(2,1)S(1)}, u32[]{:S(2)}, u32[]{:S(2)}) collective-permute-start(bf16[1024,128]{1,0:T(8,128)(2,1)S(1)} %get-tuple-element.19), channel_id=1, source_target_pairs={{0,1},{1,2},{2,3},{3,4},{4,5},{5,6},{6,7},{7,8},{8,9},{9,10},{10,1... | collective-permute-start | bytes 786440 | tf_op jit(solution)/shard_map/ppermute | solution.py:26
  4.9 12.2 %collective-permute-start.1 = (bf16[1024,128]{1,0:T(8,128)(2,1)S(1)}, bf16[1024,128]{1,0:T(8,128)(2,1)S(1)}, u32[]{:S(2)}, u32[]{:S(2)}) collective-permute-start(bf16[1024,128]{1,0:T(8,128)(2,1)S(1)} %get-tuple-element.18), channel_id=1, source_target_pairs={{1,0},{2,1},{3,2},{4,3},{5,4},{6,5},{7,6},{8,7},{9,8},{10,9},{11,1... | collective-permute-start | bytes 786440 | tf_op jit(solution)/shard_map/ppermute | solution.py:26
  13.8 1.3 copy-start.2
  13.8 1.9 %copy-start.3 = (s32[1,512]{1,0:T(1,128)S(1)}, s32[1,512]{1,0:T(1,128)}, u32[]{:S(2)}) copy-start(s32[1,512]{1,0:T(1,128)} %param.17) | copy-start | bytes 6148
  13.8 1.9 %copy-start.4 = (s32[1,512]{1,0:T(1,128)S(1)}, s32[1,512]{1,0:T(1,128)}, u32[]{:S(2)}) copy-start(s32[1,512]{1,0:T(1,128)} %param.18) | copy-start | bytes 6148
  17.1 0.7 copy-start
  17.1 0.8 copy-start.1
